TPU v7x, 32 devices: a whole 2x2x4 slice. The times are simulated.
32 devices in a mesh: dp: 32 (over z, y, x, core).
Axes of the slice: x: 2, y: 2, z: 4, core: 2. Of those that a mesh axis runs over, the one named last changes fastest.
Arguments:
- tokens: bfloat16 [25600, 768], P('dp'), may hold values from -6 to 6
- mask_bits: int32 [25600], P('dp'), may hold values 0 or 1
- groups: int32 [256], P('dp'), may hold values from 0 to 2, as said below
- offsets: int32 [256], P('dp'), may hold values from 0 to 800, as said below
- mask_token: bfloat16 [768], P('dp'), may hold values from -5 to 5
- ln1_gain: bfloat16 [768], P('dp'), may hold values from 0.099609375 to 1.8984375
- ln1_bias: bfloat16 [768], P('dp'), may hold values from -1.5 to 1.5
- w_qkv: bfloat16 [768, 2304], P('dp'), may hold values from -0.21875 to 0.21875
- b_qv: bfloat16 [1536], P('dp'), may hold values from -1.5 to 1.5
- w_proj: bfloat16 [768, 768], P('dp'), may hold values from -0.875 to 0.875
- b_proj: bfloat16 [768], P('dp'), may hold values from -1.5 to 1.5
- ln2_gain: bfloat16 [768], P('dp'), may hold values from 0.099609375 to 1.8984375
- ln2_bias: bfloat16 [768], P('dp'), may hold values from -1.5 to 1.5
- w_fc1: bfloat16 [768, 3072], P('dp'), may hold values from -0.21875 to 0.21875
- b_fc1: bfloat16 [3072], P('dp'), may hold values from -1.5 to 1.5
- w_fc2: bfloat16 [3072, 768], P('dp'), may hold values from -0.109375 to 0.109375
- b_fc2: bfloat16 [768], P('dp'), may hold values from -1.5 to 1.5
- cotangent: bfloat16 [25600, 768], P('dp'), may hold values from -6 to 6
Outputs:
- output: bfloat16 [25600, 768], P('dp')
- grad_tokens: float32 [25600, 768], P('dp')
- grad_mask_token: float32 [768], P('dp')
- grad_ln1_gain: float32 [768], P('dp')
- grad_ln1_bias: float32 [768], P('dp')
- grad_w_qkv: float32 [768, 2304], P('dp')
- grad_b_qv: float32 [1536], P('dp')
- grad_w_proj: float32 [768, 768], P('dp')
- grad_b_proj: float32 [768], P('dp')
- grad_ln2_gain: float32 [768], P('dp')
- grad_ln2_bias: float32 [768], P('dp')
- grad_w_fc1: float32 [768, 3072], P('dp')
- grad_b_fc1: float32 [3072], P('dp')
- grad_w_fc2: float32 [3072, 768], P('dp')
- grad_b_fc2: float32 [768], P('dp')
Inputs may be any that keep to these rules, and one draw needn't show every extreme that they name: `groups`: each device's 8 slots all carry one size group; which group a device gets varies with the seed, and every group occurs. `offsets`: each device's images lie back to back from its first local row, as many as fit in 800 rows; a slot without an image has offset 800.
All inputs are finite; a program needn't handle non-finite values. No bound on the sum of `mask_bits` on one device may be relied on, other than what follows from the above.
Results may differ from a plain program's by a relative error of at most 0.011.
Values may be sent and summed in bfloat16 or wider, within the bound.
A program may use at most 192 MiB of HBM per device.

v0:
```python
import functools

import jax
import jax.numpy as jnp
from jax import lax
from jax.experimental import pallas as pl
from jax.experimental.pallas import tpu as pltpu
from jax.sharding import PartitionSpec as P

P_SMALL = 100
P_MID = 196
P_LARGE = 400
eps_norm = 1e-06

def nt(a,b): return lax.dot_general(a,b,(((1,),(1,)),((),())),preferred_element_type=jnp.float32)
def nn(a,b): return lax.dot_general(a,b,(((1,),(0,)),((),())),preferred_element_type=jnp.float32)
def tn(a,b): return lax.dot_general(a,b,(((0,),(0,)),((),())),preferred_element_type=jnp.float32)

def attn_fwd_kernel(bias_ref, q_ref, k_ref, v_ref, ctx_ref, p_ref):
    q=q_ref[...]; k=k_ref[...]; v=v_ref[...]
    rows,width=q.shape
    lane=lax.broadcasted_iota(jnp.int32,(rows,width),1)
    bias=bias_ref[0]
    outs=[]
    for j in range(2):
        mine=(lane>=64)==(j==1)
        qj=jnp.where(mine,q,jnp.zeros_like(q))
        s=nt(qj,k)*0.18033688011112042+bias
        m=jnp.max(s,axis=1,keepdims=True)
        e=jnp.exp2(s-m)
        l=jnp.sum(e,axis=1,keepdims=True)
        p=(e*(1.0/l)).astype(jnp.bfloat16)
        p_ref[0,0,j]=p
        outs.append(nn(p,v))
    ctx_ref[...]=jnp.where(lane<64,outs[0],outs[1]).astype(jnp.bfloat16)

def attn_fwd(proj,bias):
    rows=proj.shape[0]; half=rows//2; width=proj.shape[1]//3; pairs=width//128
    return pl.pallas_call(attn_fwd_kernel,grid=(2,pairs),
        in_specs=[pl.BlockSpec((1,half,half),lambda b,p:(b,0,0)),
                  pl.BlockSpec((half,128),lambda b,p:(b,p)),
                  pl.BlockSpec((half,128),lambda b,p:(b,p+pairs)),
                  pl.BlockSpec((half,128),lambda b,p:(b,p+2*pairs))],
        out_specs=[pl.BlockSpec((half,128),lambda b,p:(b,p)),
                   pl.BlockSpec((1,1,2,half,half),lambda b,p:(b,p,0,0,0))],
        out_shape=[jax.ShapeDtypeStruct((rows,width),jnp.bfloat16),
                   jax.ShapeDtypeStruct((2,pairs,2,half,half),jnp.bfloat16)],
        compiler_params=pltpu.CompilerParams(vmem_limit_bytes=40<<20),name="attn_fwd")(bias,proj,proj,proj)

def attn_bwd_kernel(q_ref,k_ref,v_ref,g_ref,c_ref,p_ref,dq_ref,dk_ref,dv_ref):
    q=q_ref[...]; k=k_ref[...]; v=v_ref[...]; g=g_ref[...]; c=c_ref[...]
    rows,width=q.shape
    lane=lax.broadcasted_iota(jnp.int32,(rows,width),1)
    gc=g.astype(jnp.float32)*c.astype(jnp.float32)
    dq=[];dk=[];dv=[]
    for j in range(2):
        mine=(lane>=64)==(j==1)
        zero=jnp.zeros_like(q)
        qj=jnp.where(mine,q,zero); gj=jnp.where(mine,g,zero)
        di=jnp.sum(jnp.where(mine,gc,0.0),axis=1,keepdims=True)
        p=p_ref[0,0,j]
        dp=nt(gj,v)
        ds=(p.astype(jnp.float32)*(dp-di)).astype(jnp.bfloat16)
        dq.append(nn(ds,k))
        dk.append(tn(ds,qj))
        dv.append(tn(p,gj))
    dq_ref[...]=(jnp.where(lane<64,dq[0],dq[1])*0.125).astype(jnp.bfloat16)
    dk_ref[...]=((dk[0]+dk[1])*0.125).astype(jnp.bfloat16)
    dv_ref[...]=(dv[0]+dv[1]).astype(jnp.bfloat16)

def attn_bwd(proj,gctx,ctx,p):
    rows=proj.shape[0]; half=rows//2; width=proj.shape[1]//3; pairs=width//128
    sp=lambda o: pl.BlockSpec((half,128),lambda b,p:(b,p+o*pairs))
    return pl.pallas_call(attn_bwd_kernel,grid=(2,pairs),
        in_specs=[sp(0),sp(1),sp(2),sp(0),sp(0),pl.BlockSpec((1,1,2,half,half),lambda b,p:(b,p,0,0,0))],
        out_specs=[sp(0)]*3,
        out_shape=[jax.ShapeDtypeStruct((rows,width),jnp.bfloat16)]*3,
        compiler_params=pltpu.CompilerParams(vmem_limit_bytes=40<<20),name="attn_bwd")(proj,proj,proj,gctx,ctx,p)
MESH=pl.DeviceIdType.MESH
F32=jnp.float32; BF=jnp.bfloat16

def place():
    me=lax.axis_index("dp")
    c=lax.rem(me,2); x=lax.rem(me//2,2); y=lax.rem(me//4,2); z=me//8
    return c,x,y,z
def dev(z,yx,c): return ((z*4+yx)*2+c,)

def greet():
    c,x,y,z=place(); yx=y*2+x
    bar=pltpu.get_barrier_semaphore()
    peers=[dev(z,yx,1-c),dev(z,y*2+1-x,c),dev(z,(1-y)*2+x,c)]+[dev(lax.rem(z+k,4),yx,c) for k in (1,2,3)]
    for p in peers: pl.semaphore_signal(bar,inc=1,device_id=p,device_id_type=MESH)
    pl.semaphore_wait(bar,len(peers))

class Gather:
    def __init__(self,view,ss,rs):
        self.view=view; self.ss=ss; self.rs=rs
        c,x,y,z=place()
        self.c=c; self.z=z; self.yx=y*2+x
        self.xn=y*2+1-x; self.yn=(1-y)*2+x; self.dg=(1-y)*2+1-x
        self.sends=[]
    def _cp(self,src,dst,slot,d):
        return pltpu.make_async_remote_copy(src_ref=src,dst_ref=dst,send_sem=self.ss.at[slot],recv_sem=self.rs.at[slot],device_id=d,device_id_type=MESH)
    def send(self,src,dst,slot,d):
        cp=self._cp(src,dst,slot,d); cp.start(); self.sends.append(cp)
    def got(self,dst,slot,d):
        self._cp(dst,dst,slot,d).wait_recv()
    def one(self,z): return self.view(pl.ds(z,1),self.yx,self.c)
    def z_send(self,src):
        for k in (1,2,3):
            self.send(src,self.one(self.z),k-1,dev(lax.rem(self.z+k,4),self.yx,self.c))
    def sib(self,ref,slot): self.send(ref,ref,slot,dev(self.z,self.yx,1-self.c))
    def z_recv(self):
        for k in (1,2,3):
            zz=lax.rem(self.z+4-k,4)
            self.got(self.one(zz),k-1,dev(zz,self.yx,self.c))
    def xy_send(self):
        r=self.view(pl.ds(0,4),self.yx,self.c)
        self.send(r,r,3,dev(self.z,self.xn,self.c))
        self.send(r,r,4,dev(self.z,self.yn,self.c))
        for k in (1,2,3): self.sib(self.one(lax.rem(self.z+4-k,4)),6+k)
    def xy_recv(self):
        rx=self.view(pl.ds(0,4),self.xn,self.c)
        self.got(rx,3,dev(self.z,self.xn,self.c))
        h=self.view(pl.ds(0,2),self.xn,self.c)
        self.send(h,h,5,dev(self.z,self.yn,self.c))
        ry=self.view(pl.ds(0,4),self.yn,self.c)
        self.got(ry,4,dev(self.z,self.yn,self.c))
        h=self.view(pl.ds(2,2),self.yn,self.c)
        self.send(h,h,6,dev(self.z,self.xn,self.c))
        self.sib(rx,10); self.sib(ry,11)
    def diag_recv(self):
        a=self.view(pl.ds(0,2),self.dg,self.c)
        self.got(a,5,dev(self.z,self.yn,self.c))
        self.sib(a,12)
        b=self.view(pl.ds(2,2),self.dg,self.c)
        self.got(b,6,dev(self.z,self.xn,self.c))
        self.sib(b,13)
    def finish(self):
        o=1-self.c; s=dev(self.z,self.yx,o)
        for k in (1,2,3): self.got(self.view(pl.ds(lax.rem(self.z+4-k,4),1),self.yx,o),6+k,s)
        self.got(self.view(pl.ds(0,4),self.xn,o),10,s)
        self.got(self.view(pl.ds(0,4),self.yn,o),11,s)
        self.got(self.view(pl.ds(0,2),self.dg,o),12,s)
        self.got(self.view(pl.ds(2,2),self.dg,o),13,s)
    def drain(self):
        for cp in self.sends: cp.wait_send()

def cols_view(ref):
    half=ref.shape[-1]//2
    def view(zs,yx,lane): return ref.at[zs,yx,:,pl.ds(pl.multiple_of(lane*half,128),half)]
    return view
def rows_view(ref):
    def view(zs,yx,lane): return ref.at[zs,yx,lane]
    return view

def join(c,own,sib):
    a=own.astype(F32); b=sib.astype(F32)
    return jnp.concatenate([jnp.where(c==0,a,b),jnp.where(c==0,b,a)],axis=0).astype(BF)

def gather_kernel(sm_ref,q_ref,p_ref,f1_ref,f2_ref,gs_ref,gq_ref,gp_ref,g1_ref,g2_ref,
        sq,sp,s1,bq,bp,b1,ss0,rs0,ssl,ss,rs):
    greet()
    c,x,y,z=place(); yx=y*2+x
    sibd=dev(z,yx,1-c)
    first=[]
    def swap(src,dst,i):
        cp=pltpu.make_async_remote_copy(src_ref=src,dst_ref=dst,send_sem=ss0.at[i],recv_sem=rs0.at[i],device_id=sibd,device_id_type=MESH)
        cp.start(); first.append(cp)
    swap(sm_ref,gs_ref.at[z,yx,c],0)
    swap(q_ref,sq,1); swap(p_ref,sp,2); swap(f1_ref,s1,3)
    swap(f2_ref,g2_ref.at[z,yx,c],4)
    gs=[Gather(rows_view(gs_ref),ss.at[0],rs.at[0]),Gather(cols_view(gq_ref),ss.at[1],rs.at[1]),Gather(cols_view(gp_ref),ss.at[2],rs.at[2]),
        Gather(cols_view(g1_ref),ss.at[3],rs.at[3]),Gather(rows_view(g2_ref),ss.at[4],rs.at[4])]
    local=[]
    def keep(src,dst,i):
        cp=pltpu.make_async_copy(src,dst,ssl.at[i]); cp.start(); local.append(cp)
    def half(b):
        h=b.shape[-1]//2
        return b.at[:,:,pl.ds(pl.multiple_of(c*h,128),h)]
    keep(sm_ref,gs_ref.at[z,yx,c],0)
    keep(f2_ref,g2_ref.at[z,yx,c],4)
    def begin(i):
        if i==0:
            local[0].wait(); gs[0].z_send(gs[0].one(z))
        elif i==4:
            local[1].wait(); gs[4].z_send(gs[4].one(z))
        else:
            own,sib,buf,dst={1:(q_ref,sq,bq,gq_ref),2:(p_ref,sp,bp,gp_ref),3:(f1_ref,s1,b1,g1_ref)}[i]
            first[i].wait_recv()
            buf[0]=join(c,own[...],sib[...])
            keep(buf,dst.at[pl.ds(z,1),yx],i)
            gs[i].z_send(half(buf))
    begin(0); begin(1)
    gs[0].z_recv(); gs[0].xy_send()
    begin(2)
    gs[1].z_recv(); local[2].wait(); gs[1].xy_send()
    begin(3)
    gs[0].xy_recv()
    gs[2].z_recv(); local[3].wait(); gs[2].xy_send()
    gs[0].diag_recv()
    gs[1].xy_recv()
    begin(4)
    gs[3].z_recv(); local[4].wait(); gs[3].xy_send()
    gs[2].xy_recv()
    gs[1].diag_recv()
    gs[2].diag_recv()
    gs[4].z_recv(); gs[4].xy_send()
    gs[3].xy_recv()
    gs[3].diag_recv()
    gs[4].xy_recv()
    gs[4].diag_recv()
    first[0].wait_recv(); first[4].wait_recv()
    for g in gs: g.finish()
    for cp in first: cp.wait_send()
    for g in gs: g.drain()

def gather_all(small,wq,wp,w1,w2):
    sds=jax.ShapeDtypeStruct
    nq,np_,n1,n2=wq.shape[1],wp.shape[1],w1.shape[1],w2.shape[1]
    r=wq.shape[0]; r2=w2.shape[0]
    V=pl.BlockSpec(memory_space=pltpu.VMEM); A=pl.BlockSpec(memory_space=pl.ANY)
    D=pltpu.SemaphoreType.DMA
    return pl.pallas_call(gather_kernel,
        in_specs=[V]*5,out_specs=[A]*5,
        out_shape=[sds((4,4,2)+small.shape,BF),sds((4,4,2*r,nq),BF),sds((4,4,2*r,np_),BF),sds((4,4,2*r,n1),BF),sds((4,4,2,r2,n2),BF)],
        scratch_shapes=[pltpu.VMEM((r,n),BF) for n in (nq,np_,n1)]+[pltpu.VMEM((1,2*r,n),BF) for n in (nq,np_,n1)]+
            [D((5,)),D((5,)),D((5,)),D((5,14)),D((5,14))],
        compiler_params=pltpu.CompilerParams(collective_id=0,has_side_effects=True,vmem_limit_bytes=16<<20),name="gather_all")(small,wq,wp,w1,w2)

class Scatter:
    def __init__(self,view,a,s,rxa,ryb,rx,ry,b,rz,ss,rs,ls):
        self.view=view; self.a=a; self.s=s; self.rxa=rxa; self.ryb=ryb; self.rx=rx; self.ry=ry; self.b=b; self.rz=rz
        self.ss=ss; self.rs=rs; self.ls=ls
        c,x,y,z=place()
        self.c=c; self.z=z; self.yx=y*2+x
        self.xn=y*2+1-x; self.yn=(1-y)*2+x; self.dg=(1-y)*2+1-x
        self.cps={}
    def send(self,src,dst,slot,d):
        cp=pltpu.make_async_remote_copy(src_ref=src,dst_ref=dst,send_sem=self.ss.at[slot],recv_sem=self.rs.at[slot],device_id=d,device_id_type=MESH)
        cp.start(); self.cps[slot]=cp
    def r0(self):
        self.send(self.view(1-self.c),self.s,0,dev(self.z,self.yx,1-self.c))
        self.loc=pltpu.make_async_copy(self.view(self.c),self.a,self.ls); self.loc.start()
    def r1(self):
        self.loc.wait(); self.cps[0].wait_recv()
        a,s=self.a,self.s
        def add(yx):
            def body(i,_):
                a[i,yx]=(a[i,yx].astype(F32)+s[i,yx].astype(F32)).astype(a.dtype)
                return 0
            lax.fori_loop(0,4,body,0)
        xd=dev(self.z,self.xn,self.c); yd=dev(self.z,self.yn,self.c)
        add(self.dg)
        self.send(a.at[pl.ds(0,2),self.dg],self.rxa,1,xd)
        self.send(a.at[pl.ds(2,2),self.dg],self.ryb,2,yd)
        add(self.xn)
        self.send(a.at[pl.ds(0,2),self.xn],self.rx.at[pl.ds(0,2)],3,xd)
        add(self.yn)
        self.send(a.at[pl.ds(2,2),self.yn],self.ry.at[pl.ds(2,2)],4,yd)
        add(self.yx)
    def r2(self):
        a=self.a
        xd=dev(self.z,self.xn,self.c); yd=dev(self.z,self.yn,self.c)
        self.cps[1].wait_recv()
        def body(i,_):
            a[i,self.yn]=(a[i,self.yn].astype(F32)+self.rxa[i].astype(F32)).astype(a.dtype)
            return 0
        lax.fori_loop(0,2,body,0)
        self.send(a.at[pl.ds(0,2),self.yn],self.ry.at[pl.ds(0,2)],6,yd)
        self.cps[2].wait_recv()
        def body(i,_):
            a[i+2,self.xn]=(a[i+2,self.xn].astype(F32)+self.ryb[i].astype(F32)).astype(a.dtype)
            return 0
        lax.fori_loop(0,2,body,0)
        self.send(a.at[pl.ds(2,2),self.xn],self.rx.at[pl.ds(2,2)],5,xd)
    def r3(self):
        for s in (3,4,5,6): self.cps[s].wait_recv()
        def body(i,_):
            self.b[i]=(self.a[i,self.yx].astype(F32)+self.rx[i].astype(F32)+self.ry[i].astype(F32)).astype(self.b.dtype)
            return 0
        lax.fori_loop(0,4,body,0)
        for k in (1,2,3):
            zz=lax.rem(self.z+k,4)
            self.send(self.b.at[zz],self.rz.at[k-1],6+k,dev(zz,self.yx,self.c))
    def r4(self):
        t=self.b[self.z].astype(F32)
        for k in (1,2,3):
            self.cps[6+k].wait_recv()
            t=t+self.rz[k-1].astype(F32)
        return t
    def drain(self):
        for cp in self.cps.values(): cp.wait_send()

def scatter_scratch(r,n,dt):
    V=pltpu.VMEM
    return [V((4,4,r,n),dt),V((4,4,r,n),dt),V((2,r,n),dt),V((2,r,n),dt),V((4,r,n),dt),V((4,r,n),dt),V((4,r,n),dt),V((3,r,n),dt)]

def scatter_kernel(sm_ref,q_ref,p_ref,f1_ref,f2_ref,os_ref,oq_ref,op_ref,o1_ref,o2_ref,*sc):
    bufs=[sc[8*i:8*i+8] for i in range(5)]
    fin=sc[40:46]; ss,rs,ls,fs,fr=sc[46:]
    greet()
    c,x,y,z=place(); yx=y*2+x
    def cv(ref):
        h=ref.shape[-1]//2
        return lambda lane: ref.at[:,:,:,pl.ds(pl.multiple_of(lane*h,128),h)]
    def rv(ref): return lambda lane: ref.at[:,:,lane]
    refs=[sm_ref,q_ref,p_ref,f1_ref,f2_ref]
    S=[Scatter((rv if i in (0,4) else cv)(refs[i]),*bufs[i],ss.at[i],rs.at[i],ls.at[i]) for i in range(5)]
    order=[4,3,2,1,0]
    sibd=dev(z,yx,1-c)
    ends=[]
    outs={1:oq_ref,2:op_ref,3:o1_ref}
    def end(i):
        t=S[i].r4()
        if i==0: os_ref[...]=t
        elif i==4: o2_ref[...]=t
        else:
            f,rf=fin[2*(i-1)],fin[2*(i-1)+1]
            r=t.shape[0]//2
            f[0]=t[:r]; f[1]=t[r:]
            cp=pltpu.make_async_remote_copy(src_ref=f.at[1-c],dst_ref=rf,send_sem=fs.at[i],recv_sem=fr.at[i],device_id=sibd,device_id_type=MESH)
            cp.start(); ends.append((i,cp))
    def close():
        for i,cp in ends:
            cp.wait_recv()
            f,rf=fin[2*(i-1)],fin[2*(i-1)+1]
            own=f[c]; oth=rf[...]
            o=outs[i]; h=own.shape[-1]
            o[:,:h]=jnp.where(c==0,own,oth); o[:,h:]=jnp.where(c==0,oth,own)
            cp.wait_send()
    for i in order: S[i].r0()
    n=len(order)
    stages=[lambda i:S[i].r1(),lambda i:S[i].r2(),lambda i:S[i].r3(),lambda i:end(i)]
    for t in range(n+3):
        for s in range(3,-1,-1):
            k=t-s
            if 0<=k<n: stages[s](order[k])
    close()
    for s in S: s.drain()

def scatter_all(sm,q,p,f1,f2):
    sds=jax.ShapeDtypeStruct
    V=pl.BlockSpec(memory_space=pltpu.VMEM); A=pl.BlockSpec(memory_space=pl.ANY)
    D=pltpu.SemaphoreType.DMA
    sc=[]
    for a,dt in ((sm,F32),(q,BF),(p,BF),(f1,BF),(f2,BF)):
        if a.ndim==5: sc+=scatter_scratch(a.shape[3],a.shape[4],dt)
        else: sc+=scatter_scratch(a.shape[2],a.shape[3]//2,dt)
    outs=[sds(sm.shape[3:],F32)]
    for a in (q,p,f1):
        r,n=a.shape[2]//2,a.shape[3]
        sc+=[pltpu.VMEM((2,r,n//2),F32),pltpu.VMEM((r,n//2),F32)]
        outs.append(sds((r,n),F32))
    outs.append(sds(f2.shape[3:],F32))
    return pl.pallas_call(scatter_kernel,in_specs=[A]*5,out_specs=[V]*5,out_shape=outs,
        scratch_shapes=sc+[D((5,10)),D((5,10)),D((5,)),D((5,)),D((5,))],
        compiler_params=pltpu.CompilerParams(collective_id=1,has_side_effects=True,vmem_limit_bytes=56<<20),name="scatter_all")(sm,q,p,f1,f2)
class Gather2:
    def __init__(self,view,ss,rs):
        self.view=view; self.ss=ss; self.rs=rs
        c,x,y,z=place()
        self.c=c; self.z=z; self.yx=y*2+x
        self.xn=y*2+1-x; self.yn=(1-y)*2+x; self.dg=(1-y)*2+1-x
        self.xd=dev(z,self.xn,c); self.yd=dev(z,self.yn,c); self.sd=dev(z,self.yx,1-c)
        self.sends=[]
    def at(self,k,yx,lane=None): return self.view(pl.ds(lax.rem(self.z+4-k,4),1),yx,self.c if lane is None else lane)
    def all(self,yx,lane=None): return self.view(pl.ds(0,4),yx,self.c if lane is None else lane)
    def _cp(self,src,dst,slot,d):
        return pltpu.make_async_remote_copy(src_ref=src,dst_ref=dst,send_sem=self.ss.at[slot],recv_sem=self.rs.at[slot],device_id=d,device_id_type=MESH)
    def send(self,src,dst,slot,d):
        cp=self._cp(src,dst,slot,d); cp.start(); self.sends.append(cp)
    def got(self,dst,slot,d): self._cp(dst,dst,slot,d).wait_recv()
    def near(self,src):
        self.send(src,self.at(0,self.yx),3,self.xd)
        self.send(src,self.at(0,self.yx),7,self.yd)
    def far(self,src):
        for k in (1,2,3): self.send(src,self.at(0,self.yx),k-1,dev(lax.rem(self.z+k,4),self.yx,self.c))
    def X0(self):
        r=self.at(0,self.xn); self.got(r,3,self.xd)
        self.send(r,r,11,self.yd)
        self.got(self.at(0,self.yn),7,self.yd)
    def Z(self,k):
        r=self.at(k,self.yx)
        self.got(r,k-1,dev(lax.rem(self.z+4-k,4),self.yx,self.c))
        self.send(r,r,3+k,self.xd); self.send(r,r,7+k,self.yd); self.send(r,r,14+k,self.sd)
    def X(self,k):
        a=self.at(k,self.xn); b=self.at(k,self.yn)
        self.got(a,3+k,self.xd)
        if k==1: self.send(a,a,11+k,self.yd)
        self.got(b,7+k,self.yd)
        if k!=1: self.send(b,b,11+k,self.xd)
        if k==2:
            for yx,s in ((self.xn,18),(self.yn,19)):
                r=self.all(yx); self.send(r,r,s,self.sd)
    def D(self):
        for k in (0,1,3,2):
            self.got(self.at(k,self.dg),11+k,self.yd if k<2 else self.xd)
        r=self.all(self.dg); self.send(r,r,20,self.sd)
    def F(self):
        o=1-self.c
        for k in (1,2,3): self.got(self.at(k,self.yx,o),14+k,self.sd)
        for yx,s in ((self.xn,18),(self.yn,19),(self.dg,20)): self.got(self.all(yx,o),s,self.sd)
    def drain(self):
        for cp in self.sends: cp.wait_send()

def gelu_parts(x):
    d=1.0+0.23164189*jnp.abs(x)
    t=pl.reciprocal(d,approx=True)
    t=t*(2.0-d*t)
    e=jnp.exp2(x*x*(-0.5*1.4426950408889634))
    q=((((0.5*1.061405429*t-0.5*1.453152027)*t+0.5*1.421413741)*t-0.5*0.284496736)*t+0.5*0.254829592)*t*e
    cdf=jnp.where(x>=0,1.0-q,q)
    return x*cdf, cdf+x*e*0.3989422804014327

def row_stats(x):
    inv=1.0/x.shape[1]
    mean=jnp.sum(x,axis=1,keepdims=True)*inv
    c=x-mean
    var=jnp.sum(c*c,axis=1,keepdims=True)*inv
    return c,lax.rsqrt(var+eps_norm)

def spread(each,total,cols):
    j=lax.broadcasted_iota(jnp.int32,(128,total),1); l=lax.broadcasted_iota(jnp.int32,(128,total),0)
    return jnp.where(j-cols*each==l,1.0,0.0).astype(BF)

def over(each,shape):
    j=lax.broadcasted_iota(jnp.int32,shape,1)
    return (j*((1<<22)//each+1))>>22

def settled(g1,r):
    return r+jnp.where(r>=400,-8*g1,jnp.where(r>=392,400*g1,0))

def segments(groups,offsets,pos):
    g=groups[0]
    length=jnp.where(g==0,P_SMALL,jnp.where(g==1,P_MID,P_LARGE))
    seg=jnp.full(pos.shape,-1,jnp.int32)
    for s in range(8):
        o=offsets[s]
        seg=jnp.where((pos>=o)&(pos<o+length),s,seg)
    return seg

def settle_rows(g1,read,write):
    def either(a,b): return [jnp.where(g1==1,u,w) for u,w in zip(a,b)]
    def body(i,_):
        r=pl.multiple_of(i*56,8)
        write(r,56,read(r,56)); return 0
    lax.fori_loop(0,7,body,0)
    write(392,8,either(read(792,8),read(392,8)))
    def body2(i,_):
        r=pl.multiple_of(400+i*40,8)
        write(r,40,either(read(pl.multiple_of(392+i*40,8),40),read(r,40))); return 0
    lax.fori_loop(0,10,body2,0)

FORWARD_ORDER=(
    96, 0, 1, 16, 48, 97, 17, 64, 200, 49, 98, 32, 3, 5, 4, 20, 19, 99, 33, 21, 201, 65, 52, 2, 53, 8, 100, 6, 18,
    51, 202, 7, 24, 203, 22, 37, 36, 56, 50, 23, 35, 9, 34, 204, 10, 220, 40, 54, 55, 25, 38, 39, 80, 230, 26, 81,
    57, 41, 69, 67, 231, 68, 221, 232, 42, 66, 58, 72, 233, 222, 70, 71, 234, 85, 84, 235, 83, 82, 73, 205, 74,
    240, 241, 88, 242, 243, 86, 244, 87, 245, 250, 251, 89, 252, 253, 90,
)

def forward_kernel(groups,offsets,v0,v1,v2,v3,v4,v5,v6,v7,v8,q_ref,p_ref,f1_ref,f2_ref,tok_ref,cot_ref,mask_ref,
        wq_o,wp_o,w1_o,w2_o,pr_o,n1_o,n2_o,ctx_o,pj_o,hid_o,dg_o,st_o,mid_o,pt2_o,gt_o,cs_o,vec_o,meta_o,
        gs,gq,gp,g1w,sq,sp,s1,bq,bp,b1,raw,mid,st,n1,nt_,pj,bias,ctx,n2,hid,dg,gt,cs,pt2,pst,sc,sm_ref,smf,mk,bqv,bf1,
        ss0,rs0,ssl,sss,srs,ss,rs,psem,osem):
    smf[...]=jnp.zeros_like(smf)
    for i,r in enumerate((v0,v1,v2,v3,v4,v5,v6,v7,v8)):
        m=r.shape[0]
        smf[i:i+1,0:m]=r[...].astype(F32).reshape(1,m)
    sm_ref[...]=smf[...].astype(BF)
    greet()
    c,x,y,z=place(); yx=y*2+x
    sibd=dev(z,yx,1-c)
    first=[]
    def swap(src,dst,i):
        cp=pltpu.make_async_remote_copy(src_ref=src,dst_ref=dst,send_sem=ss0.at[i],recv_sem=rs0.at[i],device_id=sibd,device_id_type=MESH)
        cp.start(); first.append(cp)
    swap(sm_ref,gs.at[z,yx,c],0)
    swap(q_ref,sq,1); swap(p_ref,sp,2); swap(f1_ref,s1,3)
    swap(f2_ref,w2_o.at[z,yx,c],4)
    gs[z,yx,c]=sm_ref[...]
    own2=pltpu.make_async_copy(f2_ref,w2_o.at[z,yx,c],ssl.at[0]); own2.start()
    S=Gather(rows_view(gs),sss,srs)
    QA,QB,QC,Pj,F1=[Gather2(cols_view(r),ss.at[i],rs.at[i]) for i,r in enumerate((gq.at[0],gq.at[1],gq.at[2],gp,g1w))]
    F2=Gather2(rows_view(w2_o),ss.at[5],rs.at[5])
    outs=[]; lag=[]; used=[0]
    def put(src,dst):
        cp=pltpu.make_async_copy(src,dst,osem.at[used[0]]); cp.start(); outs.append(cp); used[0]+=1
    waited=set()
    def swapped(i):
        if i not in waited: waited.add(i); first[i].wait_recv()
    def build(own,sib,buf,dst):
        j=join(c,own,sib)
        buf[0]=j; dst[z,yx]=j
    def parts(ref,g): return jnp.concatenate([ref[:,o+256*g:o+256*g+256] for o in (0,768,1536)],axis=1)
    def half(b):
        h=b.shape[-1]//2
        return b.at[:,:,pl.ds(pl.multiple_of(c*h,128),h)]
    def near(n):
        if n=="F2": own2.wait(); F2.near(F2.at(0,yx)); return
        if n[0]=="Q":
            g="ABC".index(n[1]); swapped(1); build(parts(q_ref,g),parts(sq,g),bq.at[g],gq.at[g]); G[n].near(half(bq.at[g]))
        elif n=="P": swapped(2); build(p_ref[...],sp[...],bp,gp); Pj.near(half(bp))
        else: swapped(3); build(f1_ref[...],s1[...],b1,g1w); F1.near(half(b1))
    def far(n):
        if n=="F2": F2.far(F2.at(0,yx))
        elif n[0]=="Q": G[n].far(half(bq.at["ABC".index(n[1])]))
        else: G[n].far(half(bp if n=="P" else b1))
    G={"QA":QA,"QB":QB,"QC":QC,"P":Pj,"F1":F1,"F2":F2}
    def finish(n):
        if n=="F2": first[4].wait_recv()
        G[n].F()
        if n[0]=="Q": g="ABC".index(n[1]); put(gq.at[g],wq_o.at[g])
        elif n=="P": put(gp,wp_o)
        elif n=="F1": put(g1w,w1_o)
    def small(k):
        if k=="s": S.z_send(S.one(z))
        elif k=="Z": S.z_recv(); S.xy_send()
        elif k=="X": S.xy_recv()
        elif k=="D": S.diag_recv()
        else: first[0].wait_recv(); S.finish()
    g1=jnp.where(groups[0]==1,1,0)
    def setup(k):
        if k==0:
            raw[...]=tok_ref[...].astype(F32)
        segc=segments(groups,offsets,settled(g1,lax.broadcasted_iota(jnp.int32,(400,1),0)+400*k))
        meta_o[400*k:400*k+400,0:1]=jnp.where(segc>=0,1.0,0.0)
        segr=segments(groups,offsets,settled(g1,lax.broadcasted_iota(jnp.int32,(1,400),1)+400*k))
        bias[k]=jnp.where(segc==segr,0.0,-1e30)
    def vectors():
        X=gs[...].reshape(512,128)
        E=nn(X,spread(24,768,over(24,(128,768))))
        E=jnp.where(lax.broadcasted_iota(jnp.int32,(512,768),0)>>4==over(24,(512,768)),E,0.0).reshape(32,16,768)
        vec_o[...]=jnp.sum(E,axis=0)
        def wide(row,each,total):
            sel=jnp.where(lax.broadcasted_iota(jnp.int32,(32,512),1)==lax.broadcasted_iota(jnp.int32,(32,512),0)*16+row,1.0,0.0).astype(BF)
            e=nn(nn(sel,X).astype(BF),spread(each,total,over(each,(128,total))))
            e=jnp.where(lax.broadcasted_iota(jnp.int32,(32,total),0)==over(each,(32,total)),e,0.0)
            return jnp.sum(e,axis=0,keepdims=True)
        bqv[...]=wide(3,48,1536); bf1[...]=wide(7,96,3072)
    def norm_one():
        mask=jnp.broadcast_to(mask_ref[...].astype(F32).reshape(1,800),(8,800)).T
        mk[...]=mask[:,0:1]
        def write(r,n,v):
            t,m=v
            meta_o[pl.ds(r,n),1:2]=m
            mid[pl.ds(r,n),:]=jnp.where(m>0.0,vec_o[0:1,:],t)
        settle_rows(g1,lambda r,n:(raw[pl.ds(r,n),:],mk[pl.ds(r,n),:]),write)
        def body(i,_):
            r=pl.ds(pl.multiple_of(i*80,16),80)
            s=mid[r,:]
            st[r,:]=s.astype(BF)
            cc,rstd=row_stats(s)
            n1[r,:]=(cc*rstd*vec_o[1:2,:]+vec_o[2:3,:]).astype(BF)
            return 0
        lax.fori_loop(0,10,body,0)
        put(st,st_o)
    def cotangents():
        raw[...]=cot_ref[...].astype(F32)
        def write2(r,n,v): mid[pl.ds(r,n),:]=v[0]
        settle_rows(g1,lambda r,n:(raw[pl.ds(r,n),:],),write2)
        def body(i,_):
            r=pl.ds(pl.multiple_of(i*80,16),80)
            v=mid[r,:]
            cs[r,:]=v.astype(BF); gt[r,:]=(v*meta_o[r,0:1]).astype(BF)
            return 0
        lax.fori_loop(0,10,body,0)
        put(cs,cs_o); put(gt,gt_o)
        nt_[...]=n1[...].T
        put(nt_,n1_o)
        lag.append(outs[-1])
    def qkv(g):
        r=nn(n1[...],gq[g].reshape(768,768))
        for k,o in enumerate((0,768,1536)):
            t=r[:,256*k:256*k+256]
            if k!=1: t=t+bqv[:,384*k+256*g:384*k+256*g+256]
            pj[:,o+256*g:o+256*g+256]=t.astype(BF)
        if g==2: put(pj,pj_o)
    lane=lax.broadcasted_iota(jnp.int32,(400,128),1)
    def where_of(t):
        return lax.rem(t,4)//2,2*(t//4)+lax.rem(t,2)
    def pcopy(t):
        b,p=where_of(t)
        return pltpu.make_async_copy(pst.at[lax.rem(t,2)],pr_o.at[b*6+p],psem.at[lax.rem(t,2)])
    def attend(t,_):
        b,p=where_of(t); s=lax.rem(t,2)
        r=pl.ds(pl.multiple_of(b*400,16),400)
        cc=lambda o: pl.ds(pl.multiple_of(o+p*128,128),128)
        @pl.when(t>=2)
        def _(): pcopy(t-2).wait()
        q=pj[r,cc(0)]; k=pj[r,cc(768)]; v=pj[r,cc(1536)]
        res=[]
        for j in range(2):
            qj=jnp.where((lane>=64)==(j==1),q,jnp.zeros_like(q))
            sc[j]=nt(qj,k)
        for j in range(2):
            for i in range(10):
                u=slice(40*i,40*i+40)
                t_=sc[j,u]*0.18033688011112042+bias[b,u]
                e=jnp.exp2(t_-jnp.max(t_,axis=1,keepdims=True))
                sc[j,u]=e*(1.0/jnp.sum(e,axis=1,keepdims=True))
        for j in range(2):
            pr=sc[j].astype(BF)
            pst[s,j]=pr
            res.append(nn(pr,v))
        ctx[r,cc(0)]=jnp.where(lane<64,res[0],res[1]).astype(BF)
        pcopy(t).start()
        return 0
    def proj():
        put(ctx,ctx_o)
        wpv=gp[...].reshape(768,768)
        def body(i,_):
            r=pl.ds(pl.multiple_of(i*400,16),400)
            mid[r,:]=st[r,:].astype(F32)+meta_o[r,0:1]*(nn(ctx[r,:],wpv)+vec_o[4:5,:])
            return 0
        lax.fori_loop(0,2,body,0)
        def body(i,_):
            r=pl.ds(pl.multiple_of(i*80,16),80)
            cc,rstd=row_stats(mid[r,:])
            n2[r,:]=(cc*rstd*vec_o[5:6,:]+vec_o[6:7,:]).astype(BF)
            return 0
        lax.fori_loop(0,10,body,0)
        put(mid,mid_o)
        lag[0].wait(); outs[:]=[o for o in outs if o is not lag[0]]
        nt_[...]=n2[...].T
        put(nt_,n2_o)
    def mlp(i,_):
        cc=pl.ds(pl.multiple_of(i*512,128),512)
        a,d=gelu_parts(nn(n2[...],g1w[:,:,:,cc].reshape(768,512))+bf1[:,cc])
        hid[:,cc]=a.astype(BF); dg[:,cc]=d.astype(BF)
        return 0
    def grads(i,_):
        cc=pl.ds(pl.multiple_of(i*768,128),768)
        pt2[i]=tn(hid[:,cc],gt[...]).astype(BF).reshape(4,2,96,768)
        return 0
    chunks=("QA","QB","QC","P","F1","F2")
    k=0
    while k<len(FORWARD_ORDER):
        op=FORWARD_ORDER[k]; k+=1
        if op>=96 and op<200: small("sZXDF"[op-96])
        elif op<96:
            n=chunks[op//16]; g=G[n]; t=op%16
            if t==0: near(n)
            elif t==1: far(n)
            elif t==2: g.X0()
            elif t<6: g.Z(t-2)
            elif t<9: g.X(t-5)
            elif t==9: g.D()
            else: finish(n)
        elif op<220: (lambda:setup(0),lambda:setup(1),vectors,norm_one,cotangents,proj)[op-200]()
        elif op<230: qkv(op-220)
        else:
            a=b=op%10
            while k<len(FORWARD_ORDER) and FORWARD_ORDER[k]==op-a+b+1: b+=1; k+=1
            if op>=250:
                lax.fori_loop(a,b+1,grads,0)
                put(pt2.at[pl.ds(a,b+1-a)],pt2_o.at[pl.ds(a,b+1-a)])
            elif op<240: lax.fori_loop(2*a,2*b+2,attend,0)
            else:
                lax.fori_loop(a,b+1,mlp,0)
                if b==5:
                    put(hid,hid_o); put(dg,dg_o)
    pcopy(10).wait(); pcopy(11).wait()
    for cp in outs: cp.wait()
    for cp in first: cp.wait_send()
    for g in [S]+list(G.values()): g.drain()

def forward(groups,offsets,vectors,wq,wp,w1,w2,tok,cot,mask):
    sds=jax.ShapeDtypeStruct
    V=pl.BlockSpec(memory_space=pltpu.VMEM); A=pl.BlockSpec(memory_space=pl.ANY); M=pl.BlockSpec(memory_space=pltpu.SMEM)
    D=pltpu.SemaphoreType.DMA
    v=pltpu.VMEM
    R,W=tok.shape
    outs=[((3,4,4,48,768),BF),((4,4,48,768),BF),((4,4,48,3072),BF),((4,4,2,96,768),BF),((12,2,400,400),BF),
        ((W,R),BF),((W,R),BF),((R,W),BF),((R,3*W),BF),((R,4*W),BF),((R,4*W),BF),((R,W),BF),((R,W),F32),((4,4,2,96,768),BF),((R,W),BF),((R,W),BF),
        ((16,W),F32),((R,2),F32)]
    return pl.pallas_call(forward_kernel,
        in_specs=[M,M]+[V]*16,out_specs=[A]*16+[V,V],out_shape=[sds(*o) for o in outs],
        scratch_shapes=[v((4,4,2,16,128),BF),v((3,4,4,48,768),BF),v((4,4,48,768),BF),v((4,4,48,3072),BF),
            v((24,2304),BF),v((24,768),BF),v((24,3072),BF),v((3,1,48,768),BF),v((1,48,768),BF),v((1,48,3072),BF),
            v((R,W),F32),v((R,W),F32),v((R,W),BF),v((R,W),BF),v((W,R),BF),v((R,3*W),BF),v((2,400,400),F32),v((R,W),BF),v((R,W),BF),
            v((R,4*W),BF),v((R,4*W),BF),v((R,W),BF),v((R,W),BF),v((4,4,2,96,768),BF),v((2,2,400,400),BF),v((2,400,400),F32),v((16,128),BF),v((16,128),F32),v((800,1),F32),v((1,2*W),F32),v((1,4*W),F32),
            D((5,)),D((5,)),D((1,)),D((14,)),D((14,)),D((6,21)),D((6,21)),D((2,)),D((24,))],
        compiler_params=pltpu.CompilerParams(collective_id=0,has_side_effects=True,vmem_limit_bytes=60<<20),name="forward")(
        groups,offsets,*vectors,wq,wp,w1,w2,tok,cot,mask)

class Reduce:
    def __init__(self,give,a,s,rxa,ryb,rx,ry,b,rz,ss,rs):
        self.give=give; self.a=a; self.s=s; self.rxa=rxa; self.ryb=ryb; self.rx=rx; self.ry=ry; self.b=b; self.rz=rz
        self.ss=ss; self.rs=rs
        c,x,y,z=place()
        self.c=c; self.z=z; self.yx=y*2+x
        self.xn=y*2+1-x; self.yn=(1-y)*2+x; self.dg=(1-y)*2+1-x
        self.xd=dev(z,self.xn,c); self.yd=dev(z,self.yn,c); self.sd=dev(z,self.yx,1-c)
        self.cps={}
    def send(self,src,dst,slot,d):
        cp=pltpu.make_async_remote_copy(src_ref=src,dst_ref=dst,send_sem=self.ss.at[slot],recv_sem=self.rs.at[slot],device_id=d,device_id_type=MESH)
        cp.start(); self.cps[slot]=cp
    def r0(self): self.send(self.give,self.s,0,self.sd)
    def add(self,n,z0,yx,other):
        def body(i,_):
            t=self.a(pl.ds(i+z0,1),yx)
            t[...]=t[...]+other(i)[...]
            return 0
        lax.fori_loop(0,n,body,0)
    def r1(self):
        self.cps[0].wait_recv()
        def own(yx): self.add(4,0,yx,lambda i: self.s.at[pl.ds(i,1),yx])
        own(self.dg)
        self.send(self.a(pl.ds(0,2),self.dg),self.rxa,1,self.xd)
        self.send(self.a(pl.ds(2,2),self.dg),self.ryb,2,self.yd)
        own(self.xn)
        self.send(self.a(pl.ds(0,2),self.xn),self.rx.at[pl.ds(0,2)],3,self.xd)
        own(self.yn)
        self.send(self.a(pl.ds(2,2),self.yn),self.ry.at[pl.ds(2,2)],4,self.yd)
        own(self.yx)
    def r2(self):
        self.cps[1].wait_recv()
        self.add(2,0,self.yn,lambda i: self.rxa.at[pl.ds(i,1)])
        self.send(self.a(pl.ds(0,2),self.yn),self.ry.at[pl.ds(0,2)],6,self.yd)
        self.cps[2].wait_recv()
        self.add(2,2,self.xn,lambda i: self.ryb.at[pl.ds(i,1)])
        self.send(self.a(pl.ds(2,2),self.xn),self.rx.at[pl.ds(2,2)],5,self.xd)
    def r3(self):
        for s in (3,4,5,6): self.cps[s].wait_recv()
        def body(i,_):
            k=pl.ds(i,1)
            self.b[k]=(self.a(k,self.yx)[...].astype(F32)+self.rx[k].astype(F32)+self.ry[k].astype(F32)).astype(BF)
            return 0
        lax.fori_loop(0,4,body,0)
        for k in (1,2,3):
            zz=lax.rem(self.z+k,4)
            self.send(self.b.at[zz],self.rz.at[k-1],6+k,dev(zz,self.yx,self.c))
    def total(self):
        t=self.b[self.z].astype(F32)
        for k in (1,2,3):
            self.cps[6+k].wait_recv()
            t=t+self.rz[k-1].astype(F32)
        return t
    def drain(self):
        for cp in self.cps.values(): cp.wait_send()

def eights(v):
    return jnp.sum(v.reshape(v.shape[0]//8,8,v.shape[1]),axis=0)

class Total:
    def __init__(self,v,r,ss,rs):
        self.v=v; self.r=r; self.ss=ss; self.rs=rs; self.cps=[]
    def send(self,a,slot,d):
        cp=pltpu.make_async_remote_copy(src_ref=self.v.at[a],dst_ref=self.r.at[slot],send_sem=self.ss.at[slot],recv_sem=self.rs.at[slot],device_id=d,device_id_type=MESH)
        cp.start(); self.cps.append(cp)
    def stage(self,k):
        c,x,y,z=place(); yx=y*2+x
        if k:
            if k<4: self.cps[k-1].wait_recv(); self.v[k]=self.v[k-1]+self.r[k-1]
        if k==0: self.send(0,0,dev(z,yx,1-c))
        elif k==1: self.send(1,1,dev(z,y*2+1-x,c))
        elif k==2: self.send(2,2,dev(z,(1-y)*2+x,c))
        elif k==3:
            for h in (1,2,3): self.send(3,2+h,dev(lax.rem(z+h,4),yx,c))
        else:
            for h in (1,2,3): self.cps[2+h].wait_recv()
            self.sum=self.v[3]+self.r[3]+self.r[4]+self.r[5]
    def drain(self):
        for cp in self.cps: cp.wait_send()

BACKWARD_ORDER=(
    0, 200, 16, 240, 1, 241, 242, 243, 2, 220, 221, 32, 17, 48, 222, 223, 49, 201, 64, 33, 18, 3, 80, 202, 50, 203,
    204, 65, 96, 250, 81, 19, 34, 97, 251, 230, 112, 66, 252, 113, 51, 253, 35, 98, 67, 82, 231, 114, 128, 254,
    129, 83, 99, 255, 130, 232, 176, 144, 36, 52, 4, 115, 131, 177, 205, 178, 145, 206, 179, 207, 160, 146, 132,
    161, 116, 147, 162, 208, 163, 84, 20, 209, 100, 68, 180, 148, 164,
)

def backward_kernel(w2_r,w1_r,wp_r,wq_r,pr_r,n1_r,n2_r,ctx_r,pj_r,hid_r,dg_r,st_r,mid_r,pt2_r,gt_r,cs_r,vec,meta,
        out_o,tok_o,sm_o,oq,op_,o1,o2,
        w2,w1,wp,gp,pj,mid,gf,nt_,tmp,ctx,gt,gb,pst,acc,accb,
        a2,s2,xa2,yb2,x2,y2,b2,z2,part,sb,xab,ybb,xb,yb,bb,zb,fb,frb,vs,vr,us,ur,
        lsem,psem,osem,rss,rrs,fss,frs,vss,vrs,uss,urs):
    greet()
    c,x,y,z=place(); yx=y*2+x
    sibd=dev(z,yx,1-c)
    loads={}; held=set()
    def get(name,src,dst):
        cp=pltpu.make_async_copy(src,dst,lsem.at[len(loads)]); cp.start(); loads[name]=cp
    def have(*names):
        for n in names:
            if n not in held: held.add(n); loads[n].wait()
    C2=[Reduce(pt2_r.at[:,:,1-c,h],lambda zs,q,h=h: a2.at[h,zs,q],s2.at[h],xa2.at[h],yb2.at[h],x2.at[h],y2.at[h],b2.at[h],z2.at[h],rss.at[h],rrs.at[h]) for h in range(2)]
    def sib_at(i): return sb.at[i] if i<5 else s2.at[(i-5)//2,:,:,:,pl.ds(384*((i-5)%2),384)]
    mine=pl.ds(pl.multiple_of(c*384,128),384); theirs=pl.ds(pl.multiple_of((1-c)*384,128),384)
    CH=[Reduce(part.at[i,:,:,:,theirs],lambda zs,q,i=i: part.at[i,zs,q,:,mine],sib_at(i),xab.at[i],ybb.at[i],xb.at[i],yb.at[i],bb.at[i],zb.at[i],rss.at[2+i],rrs.at[2+i]) for i in range(8)]
    F=CH[0:4]; PJ=CH[4]; QK=CH[5:8]
    get("gt",gt_r,gt)
    get("w2a",w2_r.at[pl.ds(0,32)],w2.at[pl.ds(0,32)]); get("dga",dg_r.at[:,pl.ds(0,1536)],gp.at[:,pl.ds(0,1536)])
    get("a2a",pt2_r.at[:,:,c,0],a2.at[0])
    get("w2b",w2_r.at[pl.ds(32,32)],w2.at[pl.ds(32,32)]); get("dgb",dg_r.at[:,pl.ds(1536,1536)],gp.at[:,pl.ds(1536,1536)])
    get("a2b",pt2_r.at[:,:,c,1],a2.at[1])
    get("n2",n2_r,nt_); get("cs",cs_r,tmp)
    get("w1",w1_r,w1); get("mid",mid_r,mid); get("wp",wp_r,wp); get("ctx",ctx_r,ctx); get("pj",pj_r,pj)
    acc[...]=jnp.zeros_like(acc)
    ends=[]
    def end(i):
        t=CH[i].total()
        fb[i,0]=t[:24]; fb[i,1]=t[24:]
        cp=pltpu.make_async_remote_copy(src_ref=fb.at[i,1-c],dst_ref=frb.at[i],send_sem=fss.at[i],recv_sem=frs.at[i],device_id=sibd,device_id_type=MESH)
        cp.start(); ends.append((i,cp))
    def end2(h): o2[48*h:48*h+48,:]=C2[h].total()
    def mlp(i,_):
        cc=pl.ds(pl.multiple_of(i*768,128),768)
        g=(nt(gt[...],w2[pl.ds(16*i,16)].reshape(768,768))*gp[:,cc].astype(F32)).astype(BF)
        gp[:,cc]=g
        accb[:,cc]=eights(g.astype(F32))
        return 0
    def w1grad(i):
        have("n2")
        part[i]=nn(nt_[...],gp[:,768*i:768*i+768]).astype(BF).reshape(4,4,48,768)
        if i==3: get("n1",n1_r,nt_)
    def norm_back(i0,rows,gain,ka,kb,finish):
        def body(i,_):
            r=pl.ds(pl.multiple_of(i0+i*80,16),80)
            g,m=gf[r,:],rows(r)
            cc,rstd=row_stats(m)
            xh=cc*rstd
            acc[ka]+=eights(g*xh); acc[kb]+=eights(g)
            gx=g*gain
            m1=jnp.sum(gx,axis=1,keepdims=True)*(1.0/768); m2=jnp.sum(gx*xh,axis=1,keepdims=True)*(1.0/768)
            finish(r,rstd*(gx-m1-xh*m2))
            return 0
        lax.fori_loop(0,5,body,0)
    def finish2(r,d):
        gm=tmp[r,:].astype(F32)+d
        mid[r,:]=gm
        v=(meta[r,0:1]*gm).astype(BF)
        gb[r,:]=v
        acc[4]+=eights(v.astype(F32))
        acc[8]+=eights(gt[r,:].astype(F32))
    def p10(k):
        have("w1","cs","mid")
        r=slice(400*k,400*k+400)
        gf[r,:]=nt(gp[r,:],w1[...].reshape(768,3072))
        norm_back(400*k,lambda r: mid[r,:],vec[5:6,:],5,6,finish2)
        if k==1:
            get("hid",hid_r,gp); get("st",st_r,tmp)
            for g in range(3): get("wq%d"%g,wq_r.at[g],w1.at[:,:,:,pl.ds(768*g,768)])
    gc=gt
    def gctx():
        have("wp")
        gc[...]=nt(gb[...],wp[...].reshape(768,768)).astype(BF)
        pcopy(0).start()
    def wpgrad():
        have("ctx")
        part[4]=tn(ctx[...],gb[...]).astype(BF).reshape(4,4,48,768)
    lane=lax.broadcasted_iota(jnp.int32,(400,128),1)
    def where_of(t):
        return lax.rem(t,4)//2,2*(t//4)+lax.rem(t,2)
    def pcopy(t):
        b,p=where_of(t)
        return pltpu.make_async_copy(pr_r.at[b*6+p],pst.at[lax.rem(t,2)],psem.at[lax.rem(t,2)])
    def attend(t,_):
        b,p=where_of(t); s=lax.rem(t,2)
        r=pl.ds(pl.multiple_of(b*400,16),400)
        cc=lambda o: pl.ds(pl.multiple_of(o+p*128,128),128)
        pcopy(t).wait()
        @pl.when(t<11)
        def _(): pcopy(t+1).start()
        q=pj[r,cc(0)]; k=pj[r,cc(768)]; v=pj[r,cc(1536)]; g=gc[r,cc(0)]
        gx=g.astype(F32)*ctx[r,cc(0)].astype(F32)
        dq=[];dk=[];dv=[]
        for j in range(2):
            own=(lane>=64)==(j==1)
            zero=jnp.zeros_like(q)
            qj=jnp.where(own,q,zero); gj=jnp.where(own,g,zero)
            di=jnp.sum(jnp.where(own,gx,0.0),axis=1,keepdims=True)
            pr=pst[s,j]
            ds=(pr.astype(F32)*(nt(gj,v)-di)).astype(BF)
            dq.append(nn(ds,k)); dk.append(tn(ds,qj)); dv.append(tn(pr,gj))
        pj[r,cc(0)]=(jnp.where(lane<64,dq[0],dq[1])*0.125).astype(BF)
        pj[r,cc(768)]=((dk[0]+dk[1])*0.125).astype(BF)
        pj[r,cc(1536)]=(dv[0]+dv[1]).astype(BF)
        return 0
    def group(r,g): return jnp.concatenate([pj[r,o+256*g:o+256*g+256] for o in (0,768,1536)],axis=1)
    def qkvgrad(g):
        if g==0: have("n1")
        cols=group(slice(None),g)
        acc[3,:,256*g:256*g+256]=eights(cols[:,:256].astype(F32)); acc[7,:,256*g:256*g+256]=eights(cols[:,512:].astype(F32))
        part[5+g]=nn(nt_[...],cols).astype(BF).reshape(4,4,48,768)
        if g==2:
            for k in range(6): us[0,k:k+1,:]=jnp.sum(acc[3+k],axis=0,keepdims=True)
            for k in range(4): us[0,6+k:7+k,:]=jnp.sum(accb[:,768*k:768*k+768],axis=0,keepdims=True)
            us[0,10:16,:]=jnp.zeros((6,768),F32)
    def finish1(r,d):
        gs=mid[r,:]+d
        m=meta[r,1:2]>0.0
        acc[0]+=eights(jnp.where(m,gs,0.0))
        mid[r,:]=jnp.where(m,0.0,gs)
    stores=[]
    def put(src,dst):
        cp=pltpu.make_async_copy(src,dst,osem.at[len(stores)]); cp.start(); stores.append(cp)
    def back(i):
        if i==0: have("st","wq0","wq1","wq2")
        r=slice(400*i,400*i+400)
        gf[r,:]=sum(nt(group(r,g),w1[:,:,:,768*g:768*g+768].reshape(768,768)) for g in range(3))
        norm_back(400*i,lambda r: tmp[r,:].astype(F32),vec[1:2,:],1,2,finish1)
        if i==1: put(mid,tok_o); get("mid2",mid_r,gf)
    def fin():
        for k in range(3): vs[0,k:k+1,:]=jnp.sum(acc[k],axis=0,keepdims=True)
        vs[0,3:8,:]=jnp.zeros((5,768),F32)
    def outp(i):
        if i==0: have("hid","mid2")
        r=slice(400*i,400*i+400)
        gf[r,:]=gf[r,:]+meta[r,0:1]*(nn(gp[r,:],w2[...].reshape(3072,768))+vec[8:9,:])
        put(gf.at[pl.ds(400*i,400)],out_o.at[pl.ds(400*i,400)])
    sums=[Total(vs,vr,vss,vrs),Total(us,ur,uss,urs)]
    plain=(lambda:None,lambda:p10(0),lambda:p10(1),gctx,wpgrad,lambda:back(0),lambda:back(1),fin,lambda:outp(0),lambda:outp(1))
    k=0
    while k<len(BACKWARD_ORDER):
        op=BACKWARD_ORDER[k]; k+=1
        i,t=op//16,op%16
        if i<10:
            if t==4:
                if i<2: end2(i)
                else: end(i-2)
            else:
                if i<2 and t==1: have(("a2a","a2b")[i])
                r=(C2+CH)[i]
                (r.r0,r.r1,r.r2,r.r3)[t]()
        elif i<12: sums[i-10].stage(t)
        elif op<220: plain[op-200]()
        elif op<230: w1grad(op-220)
        elif op<240: qkvgrad(op-230)
        else:
            a=b=op%10
            while k<len(BACKWARD_ORDER) and BACKWARD_ORDER[k]==op-a+b+1: b+=1; k+=1
            if op<250:
                for i in range(a,b+1):
                    if i==0: have("gt","w2a","dga")
                    if i==2: have("w2b","dgb")
                for lo,hi in ((a,min(b+1,2)),(max(a,2),b+1)):
                    if lo<hi: lax.fori_loop(lo,hi,mlp,0)
            else:
                if a==0: have("pj")
                lax.fori_loop(2*a,2*b+2,attend,0)
    vt,ut=sums[0].sum,sums[1].sum
    me=lax.axis_index("dp")
    def turn(v,by): return pltpu.roll(v,lax.rem(768-by,768),1)[:,:128]
    eight=lambda v: jnp.concatenate([v]*8,axis=0)
    sm_o[0:8,:]=turn(vt,24*me)
    t=turn(ut,24*me)
    sm_o[4:7,:]=t[1:4]; sm_o[8:9,:]=t[5:6]
    sm_o[3:4,:]=turn(eight(jnp.where(me>=16,ut[4:5],ut[0:1])),48*lax.rem(me,16))[0:1]
    k8=me//8
    pick=jnp.where(k8==0,ut[6:7],jnp.where(k8==1,ut[7:8],jnp.where(k8==2,ut[8:9],ut[9:10])))
    sm_o[7:8,:]=turn(eight(pick),96*lax.rem(me,8))[0:1]
    for i,cp in ends:
        cp.wait_recv()
        own=fb[i,c]; oth=frb[i]
        lo=jnp.where(c==0,own,oth); hi=jnp.where(c==0,oth,own)
        if i<4: o1[:,768*i:768*i+384]=lo; o1[:,768*i+384:768*i+768]=hi
        elif i==4: op_[:,:384]=lo; op_[:,384:]=hi
        else:
            g=256*(i-5)
            oq[:,g:g+256]=lo[:,:256]; oq[:,768+g:768+g+128]=lo[:,256:]
            oq[:,768+g+128:768+g+256]=hi[:,:128]; oq[:,1536+g:1536+g+256]=hi[:,128:]
        cp.wait_send()
    for cp in stores: cp.wait()
    for q in C2+CH+sums: q.drain()

def backward(w2,w1,wp,wq,pr,n1,n2,ctx,pj,hid,dg,st,mid,pt2,gt,cs,vec,meta):
    sds=jax.ShapeDtypeStruct
    V=pl.BlockSpec(memory_space=pltpu.VMEM); A=pl.BlockSpec(memory_space=pl.ANY)
    D=pltpu.SemaphoreType.DMA
    v=pltpu.VMEM
    W,R=n1.shape
    scr=[v((64,48,W),BF),v((4,4,48,4*W),BF),v((4,4,48,W),BF),v((R,4*W),BF),v((R,3*W),BF),v((R,W),F32),v((R,W),F32),v((W,R),BF),
        v((R,W),BF),v((R,W),BF),v((R,W),BF),v((R,W),BF),v((2,2,400,400),BF),v((9,8,W),F32),v((8,4*W),F32)]
    def rs(n,r,w,own):
        o=[v((n,4,4,r,own),BF),v((min(n,5),4,4,r,w),BF),v((n,2,r,w),BF),v((n,2,r,w),BF),v((n,4,r,w),BF),v((n,4,r,w),BF),v((n,4,r,w),BF),v((n,3,r,w),BF)]
        return o
    scr+=rs(2,48,W,W)+rs(8,48,W//2,W)
    scr+=[v((8,2,24,W//2),F32),v((8,24,W//2),F32),v((4,8,W),F32),v((6,8,W),F32),v((4,16,W),F32),v((6,16,W),F32)]
    scr+=[D((24,)),D((2,)),D((3,)),D((10,10)),D((10,10)),D((8,)),D((8,))]+[D((6,))]*4
    outs=[((R,W),F32),((R,W),F32),((16,128),F32),((24,3*W),F32),((24,W),F32),((24,4*W),F32),((96,W),F32)]
    return pl.pallas_call(backward_kernel,in_specs=[A]*16+[V]*2,out_specs=[A,A]+[V]*5,out_shape=[sds(*o) for o in outs],scratch_shapes=scr,
        compiler_params=pltpu.CompilerParams(collective_id=1,has_side_effects=True,vmem_limit_bytes=63<<20),name="backward")(
        w2,w1,wp,wq,pr,n1,n2,ctx,pj,hid,dg,st,mid,pt2,gt,cs,vec,meta)

def settle_back_kernel(groups,out_r,tok_r,sm,q_r,p_r,w1_r,w2_r,out_o,tok_o,q_o,p_o,w1_o,w2_o,v0,v1,v2,v3,v4,v5,v6,v7,v8,buf,sem):
    cps=[pltpu.make_async_copy(a,b,sem.at[i]) for i,(a,b) in enumerate(((out_r,buf),(q_r,q_o),(p_r,p_o),(w1_r,w1_o),(w2_r,w2_o)))]
    for cp in cps: cp.start()
    moved=groups[0]==1
    one=[pltpu.make_async_copy(tok_r,tok_o,sem.at[5])]
    three=[pltpu.make_async_copy(tok_r.at[pl.ds(a,n)],tok_o.at[pl.ds(b,n)],sem.at[6+i]) for i,(a,b,n) in enumerate(((0,0,392),(400,392,400),(392,792,8)))]
    @pl.when(moved)
    def _():
        for cp in three: cp.start()
    @pl.when(jnp.logical_not(moved))
    def _():
        for cp in one: cp.start()
    for i,v in enumerate((v0,v1,v2,v3,v4,v5,v6,v7,v8)):
        m=v.shape[0]
        v[...]=sm[i:i+1,0:m].reshape(m)
    cps[0].wait()
    out_o[0:384]=buf[0:384].astype(BF)
    a=buf[384:800]
    b=jnp.concatenate([buf[384:392],buf[400:800],buf[392:400]],axis=0)
    out_o[384:800]=jnp.where(moved,b,a).astype(BF)
    for cp in cps[1:]: cp.wait()
    @pl.when(moved)
    def _():
        for cp in three: cp.wait()
    @pl.when(jnp.logical_not(moved))
    def _():
        for cp in one: cp.wait()

def settle_back(groups,sizes,out,tok,sm,q,p,w1,w2):
    sds=jax.ShapeDtypeStruct
    V=pl.BlockSpec(memory_space=pltpu.VMEM); A=pl.BlockSpec(memory_space=pl.ANY); M=pl.BlockSpec(memory_space=pltpu.SMEM)
    return pl.pallas_call(settle_back_kernel,in_specs=[M,A,A,V,A,A,A,A],out_specs=[V]+[A]*5+[V]*len(sizes),
        out_shape=[sds(out.shape,BF)]+[sds(a.shape,F32) for a in (tok,q,p,w1,w2)]+[sds((m,),F32) for m in sizes],
        scratch_shapes=[pltpu.VMEM(out.shape,F32),pltpu.SemaphoreType.DMA((9,))],
        compiler_params=pltpu.CompilerParams(vmem_limit_bytes=60<<20),name="settle_back")(groups,out,tok,sm,q,p,w1,w2)

def normalize(values, gain, shift):
    center = values - jnp.mean(values, axis=-1, keepdims=True)
    spread = jnp.mean(center * center, axis=-1, keepdims=True)
    return center * lax.rsqrt(spread + eps_norm) * gain + shift

def activate(values):
    return jax.nn.gelu(values, approximate=False)

def segment_rows(groups, offsets, rows):
    lengths = jnp.where(groups == 0, P_SMALL, jnp.where(groups == 1, P_MID, P_LARGE)).astype(jnp.int32)
    positions = jnp.arange(rows, dtype=jnp.int32)
    inside = (positions[None, :] >= offsets[:, None]) & (positions[None, :] < offsets[:, None] + lengths[:, None])
    labels = jnp.arange(1, offsets.shape[0] + 1, dtype=jnp.int32)
    return jnp.sum(jnp.where(inside, labels[:, None], 0), axis=0) - 1

def settle(mid, rows):
    half = rows.shape[0] // 2
    cut = P_MID * (half // P_MID)
    gap = half - cut
    end = rows.shape[0] - gap
    moved = jnp.concatenate([rows[:cut], rows[end:], rows[cut:end]], axis=0)
    return jnp.where(mid, moved, rows)

def unsettle(mid, rows):
    half = rows.shape[0] // 2
    cut = P_MID * (half // P_MID)
    gap = half - cut
    moved = jnp.concatenate([rows[:cut], rows[half:], rows[cut:half]], axis=0)
    return jnp.where(mid, moved, rows)

def shards(n, tokens, mask_bits, groups, offsets, mask_token, ln1_gain, ln1_bias, w_qkv, b_qv, w_proj, b_proj,
           ln2_gain, ln2_bias, w_fc1, b_fc1, w_fc2, b_fc2, cotangent):
    vectors = (mask_token, ln1_gain, ln1_bias, b_qv, b_proj, ln2_gain, ln2_bias, b_fc1, b_fc2)
    sizes = [v.shape[0] for v in vectors]
    places = [sum(sizes[:i]) for i in range(len(sizes) + 1)]
    small_all = lax.all_gather(jnp.concatenate(vectors), "dp", axis=0, tiled=False)
    full_qkv, full_proj, full_fc1, full_fc2 = [
        lax.all_gather(w, "dp", axis=0, tiled=True) for w in (w_qkv, w_proj, w_fc1, w_fc2)]
    token_mask, gain_one, shift_one, bias_qv, bias_proj, gain_two, shift_two, bias_one, bias_two = [
        small_all[:, places[i]:places[i + 1]].reshape(-1).astype(F32) for i in range(len(sizes))]
    rows, width = tokens.shape
    half = rows // 2
    mid = groups[0] == 1
    tokens = settle(mid, tokens)
    cotangent = settle(mid, cotangent)
    mask_bits = settle(mid, mask_bits)
    segment = settle(mid, segment_rows(groups, offsets, rows))
    valid_col = (segment >= 0).astype(F32)[:, None]
    halves = segment.reshape(2, half)
    bias = jnp.where(halves[:, :, None] == halves[:, None, :], 0.0, -1e30).astype(F32)
    masked_rows = (mask_bits == 1)[:, None]
    start = jnp.where(masked_rows, token_mask[None, :], tokens.astype(F32))
    normed_one = normalize(start, gain_one, shift_one).astype(BF)
    full_bias = jnp.concatenate([bias_qv[:width], jnp.zeros((width,), F32), bias_qv[width:]])
    projected = (jnp.dot(normed_one, full_qkv, preferred_element_type=F32) + full_bias).astype(BF)
    context_low, probs = attn_fwd(projected, bias)
    middle = start + valid_col * (jnp.dot(context_low, full_proj, preferred_element_type=F32) + bias_proj)
    normed_two = normalize(middle, gain_two, shift_two).astype(BF)
    hidden_pre = jnp.dot(normed_two, full_fc1, preferred_element_type=F32) + bias_one
    hidden_low = activate(hidden_pre).astype(BF)
    result = middle + valid_col * (jnp.dot(hidden_low, full_fc2, preferred_element_type=F32) + bias_two)
    output = unsettle(mid, result.astype(BF))
    upstream = cotangent.astype(F32)
    grad_two = (valid_col * upstream).astype(BF)
    grad_wfc2 = tn(hidden_low, grad_two)
    grad_bfc2 = jnp.sum(grad_two.astype(F32), axis=0)
    grad_hidden = nt(grad_two, full_fc2)
    _, gelu_back = jax.vjp(activate, hidden_pre)
    grad_pre = gelu_back(grad_hidden)[0].astype(BF)
    grad_wfc1 = tn(normed_two, grad_pre)
    grad_bfc1 = jnp.sum(grad_pre.astype(F32), axis=0)
    grad_normed_two = nt(grad_pre, full_fc1)
    _, norm_back_two = jax.vjp(normalize, middle, gain_two, shift_two)
    grad_mid_part, grad_gain_two, grad_shift_two = norm_back_two(grad_normed_two)
    grad_middle = upstream + grad_mid_part
    grad_branch = (valid_col * grad_middle).astype(BF)
    grad_wproj = tn(context_low, grad_branch)
    grad_bproj = jnp.sum(grad_branch.astype(F32), axis=0)
    grad_context = nt(grad_branch, full_proj).astype(BF)
    dq, dk, dv = attn_bwd(projected, grad_context, context_low, probs)
    grad_projected = jnp.concatenate([dq, dk, dv], axis=1)
    grad_wqkv = tn(normed_one, grad_projected)
    grad_bqv = jnp.concatenate([jnp.sum(dq.astype(F32), axis=0), jnp.sum(dv.astype(F32), axis=0)])
    grad_normed_one = nt(grad_projected, full_qkv)
    _, norm_back_one = jax.vjp(normalize, start, gain_one, shift_one)
    grad_start_part, grad_gain_one, grad_shift_one = norm_back_one(grad_normed_one)
    grad_start = grad_middle + grad_start_part
    grad_token = jnp.sum(jnp.where(masked_rows, grad_start, 0.0), axis=0)
    grad_input = unsettle(mid, jnp.where(masked_rows, 0.0, grad_start))
    grad_vectors = (grad_token, grad_gain_one, grad_shift_one, grad_bqv, grad_bproj, grad_gain_two, grad_shift_two,
                    grad_bfc1, grad_bfc2)
    grad_small = jnp.concatenate([g.reshape(n, -1) for g in grad_vectors], axis=1)
    small_share = lax.psum_scatter(grad_small, "dp", scatter_dimension=0, tiled=False)
    share_qkv, share_proj, share_fc1, share_fc2 = [
        lax.psum_scatter(g, "dp", scatter_dimension=0, tiled=True)
        for g in (grad_wqkv, grad_wproj, grad_wfc1, grad_wfc2)]
    v = [small_share[places[i]:places[i + 1]] for i in range(len(sizes))]
    return (output, grad_input, v[0], v[1], v[2], share_qkv, v[3], share_proj, v[4], v[5], v[6], share_fc1, v[7],
            share_fc2, v[8])


def shards_fast(n, tokens, mask_bits, groups, offsets, mask_token, ln1_gain, ln1_bias, w_qkv, b_qv, w_proj, b_proj,
           ln2_gain, ln2_bias, w_fc1, b_fc1, w_fc2, b_fc2, cotangent):
    vectors = (mask_token, ln1_gain, ln1_bias, b_qv, b_proj, ln2_gain, ln2_bias, b_fc1, b_fc2)
    sizes = [v.shape[0] for v in vectors]
    (gq, gp, g1, g2, probs, normed_one, normed_two, context_low, projected, hidden_low, dgelu, start, middle, part2,
     grad_two, cots, vec, meta) = forward(groups, offsets, vectors, w_qkv, w_proj, w_fc1, w_fc2, tokens, cotangent, mask_bits)
    width = tokens.shape[1]
    shares = backward(
        g2.reshape(64, 48, width), g1, gp, gq, probs, normed_one, normed_two, context_low,
        projected, hidden_low, dgelu, start, middle, part2.reshape(4, 4, 2, 2, 48, width), grad_two, cots, vec, meta)
    output, grad_input, share_qkv, share_proj, share_fc1, share_fc2, *v = settle_back(groups, sizes, *shares)
    return (output, grad_input, v[0], v[1], v[2], share_qkv, v[3], share_proj, v[4], v[5], v[6], share_fc1, v[7],
            share_fc2, v[8])

def solution(mesh):
    row, flat = P("dp", None), P("dp")
    return jax.shard_map(
        functools.partial(shards_fast if mesh.shape["dp"] == 32 else shards, mesh.shape["dp"]),
        mesh=mesh,
        in_specs=(row, flat, flat, flat, flat, flat, flat, row, flat, row, flat, flat, flat, row, flat, row, flat, row),
        out_specs=(row, row, flat, flat, flat, row, flat, row, flat, flat, flat, row, flat, row, flat),
        check_vma=False,
    )
```

profile of v0, /device:TPU:0, one launch (start us, length us, event | category | flops | bytes accessed | tf_op | source)
XLA Modules:
  0.0 273.6 jit_solution(15031139910828802372)
XLA Ops:
  0.7 83.1 %forward.1 = (bf16[3,4,4,48,768]{4,3,2,1,0:T(8,128)(2,1)}, bf16[4,4,48,768]{3,2,1,0:T(8,128)(2,1)}, bf16[4,4,48,3072]{3,2,1,0:T(8,128)(2,1)}, bf16[4,4,2,96,768]...) custom-call(s32[8]{0:T(128)} %groups.3, ...), custom_call_target="tpu_custom_call" | custom-call | tf_op jit(solution)/shard_map/forward/pallas_call | solution.py:677
  83.7 85.5 %backward.1 = (f32[800,768]{1,0:T(8,128)}, f32[800,768]{1,0:T(8,128)}, f32[16,128]{1,0:T(8,128)}, f32[24,2304]{1,0:T(8,128)}, f32[24,768]{1,0:T(8,128)}, /*index=5*/f32[24,3072]{1,0:T(8,128)}, f32[96,768]{1,0:T(8,128)}) custom-call(bf16[64,48,768]{2,1,0:T(8,128)(2,1)} %bitcast.2, bf16[4,4,48,3072]{3,2,1,0:T(8,128)(2,1)} %get-tuple-element.56.w1_r, ...), custom_call_target="tpu_custom_call" | custom-call | tf_op jit(solution)/shard_map/backward/pallas_call | solution.py:983
  169.2 104.2 %settle_back.1 = (bf16[800,768]{1,0:T(8,128)(2,1)}, f32[800,768]{1,0:T(8,128)}, f32[24,2304]{1,0:T(8,128)}, f32[24,768]{1,0:T(8,128)}, f32[24,3072]{1,0:T(8,128)...) custom-call(s32[8]{0:T(128)} %groups.3, ...), custom_call_target="tpu_custom_call" | custom-call | tf_op jit(solution)/shard_map/settle_back/pallas_call | solution.py:1018
where the time goes:
time: 277 us; the launch traced here: 274 us
  Pallas kernels  273 us (99%)
    pallas_call x1, Pallas kernels, settle_back(): pl.pallas_call(settle_back_kernel, in_specs=[M, A, A, V, A, A, A, A], out...  104 us
    pallas_call x1, Pallas kernels, backward(): pl.pallas_call(backward_kernel, in_specs=[A] * 16 + [V] * 2, out_specs=[A...  85.5 us
    pallas_call x1, Pallas kernels, forward(): pl.pallas_call(forward_kernel, in_specs=[M, M] + [V] * 16, out_specs=[A]...  83.1 us

commit v1 on v0

--- a/solution.py
+++ b/solution.py
@@ -405,12 +405,8 @@
         for cp in self.sends: cp.wait_send()
 
 def gelu_parts(x):
-    d=1.0+0.23164189*jnp.abs(x)
-    t=pl.reciprocal(d,approx=True)
-    t=t*(2.0-d*t)
+    cdf=0.5+0.5*lax.erf(x*0.7071067811865476)
     e=jnp.exp2(x*x*(-0.5*1.4426950408889634))
-    q=((((0.5*1.061405429*t-0.5*1.453152027)*t+0.5*1.421413741)*t-0.5*0.284496736)*t+0.5*0.254829592)*t*e
-    cdf=jnp.where(x>=0,1.0-q,q)
     return x*cdf, cdf+x*e*0.3989422804014327
 
 def row_stats(x):
@@ -419,6 +415,13 @@
     c=x-mean
     var=jnp.sum(c*c,axis=1,keepdims=True)*inv
     return c,lax.rsqrt(var+eps_norm)
+
+def by_sixteen(first,last,rows):
+    step=next(k for k in (200,160,80) if k%16==0 and (last-first)%k==0)
+    def body(i,_):
+        for u in range(step//16): rows(pl.ds(pl.multiple_of(first+i*step+16*u,16),16))
+        return 0
+    lax.fori_loop(0,(last-first)//step,body,0)
 
 def spread(each,total,cols):
     j=lax.broadcasted_iota(jnp.int32,(128,total),1); l=lax.broadcasted_iota(jnp.int32,(128,total),0)
@@ -453,16 +456,18 @@
     lax.fori_loop(0,10,body2,0)
 
 FORWARD_ORDER=(
-    96, 0, 1, 16, 48, 97, 17, 64, 200, 49, 98, 32, 3, 5, 4, 20, 19, 99, 33, 21, 201, 65, 52, 2, 53, 8, 100, 6, 18,
-    51, 202, 7, 24, 203, 22, 37, 36, 56, 50, 23, 35, 9, 34, 204, 10, 220, 40, 54, 55, 25, 38, 39, 80, 230, 26, 81,
-    57, 41, 69, 67, 231, 68, 221, 232, 42, 66, 58, 72, 233, 222, 70, 71, 234, 85, 84, 235, 83, 82, 73, 205, 74,
-    240, 241, 88, 242, 243, 86, 244, 87, 245, 250, 251, 89, 252, 253, 90,
+    96, 0, 1, 16, 32, 48, 17, 97, 200, 80, 4, 201, 98, 3, 21, 49, 5, 64, 33, 65, 99, 6, 50, 100, 2, 8, 7, 53, 20,
+    81, 202, 51, 19, 203, 24, 37, 52, 9, 35, 204, 54, 36, 56, 34, 22, 40, 18, 55, 23, 10, 220, 230, 38, 39, 69,
+    25, 231, 41, 26, 67, 68, 221, 72, 42, 66, 57, 232, 233, 222, 70, 71, 234, 85, 58, 83, 235, 84, 82, 73, 205,
+    74, 240, 88, 241, 86, 242, 243, 87, 244, 245, 250, 251, 89, 252, 253, 90,
 )
 
-def forward_kernel(groups,offsets,v0,v1,v2,v3,v4,v5,v6,v7,v8,q_ref,p_ref,f1_ref,f2_ref,tok_ref,cot_ref,mask_ref,
-        wq_o,wp_o,w1_o,w2_o,pr_o,n1_o,n2_o,ctx_o,pj_o,hid_o,dg_o,st_o,mid_o,pt2_o,gt_o,cs_o,vec_o,meta_o,
-        gs,gq,gp,g1w,sq,sp,s1,bq,bp,b1,raw,mid,st,n1,nt_,pj,bias,ctx,n2,hid,dg,gt,cs,pt2,pst,sc,sm_ref,smf,mk,bqv,bf1,
-        ss0,rs0,ssl,sss,srs,ss,rs,psem,osem):
+def forward_kernel(groups,offsets,v0,v1,v2,v3,v4,v5,v6,v7,v8,q_ref,p_ref,f1_ref,f2_ref,tok_r,cot_r,mask_ref,
+        wq_o,wp_o,w1_o,w2_o,pr_o,n1_o,n2_o,ctx_o,pj_o,hid_o,dg_o,xa_o,xb_o,mid_o,pt2_o,gt_o,cs_o,vec_o,meta_o,
+        gs,gq,gp,g1w,sq,sp,s1,bq,bp,b1,raw,mid,st,xa,xb,n1,nt_,pj,bias,ctx,n2,hid,dg,gt,cs,pt2,pst,sc,sm_ref,smf,mk,tok_ref,cot_ref,bqv,bf1,
+        ss0,rs0,ssl,sss,srs,ss,rs,psem,osem,lsem):
+    loads=[pltpu.make_async_copy(a,b,lsem.at[i]) for i,(a,b) in enumerate(((tok_r,tok_ref),(cot_r,cot_ref)))]
+    for cp in loads: cp.start()
     smf[...]=jnp.zeros_like(smf)
     for i,r in enumerate((v0,v1,v2,v3,v4,v5,v6,v7,v8)):
         m=r.shape[0]
@@ -522,6 +527,7 @@
     g1=jnp.where(groups[0]==1,1,0)
     def setup(k):
         if k==0:
+            loads[0].wait()
             raw[...]=tok_ref[...].astype(F32)
         segc=segments(groups,offsets,settled(g1,lax.broadcasted_iota(jnp.int32,(400,1),0)+400*k))
         meta_o[400*k:400*k+400,0:1]=jnp.where(segc>=0,1.0,0.0)
@@ -546,16 +552,17 @@
             meta_o[pl.ds(r,n),1:2]=m
             mid[pl.ds(r,n),:]=jnp.where(m>0.0,vec_o[0:1,:],t)
         settle_rows(g1,lambda r,n:(raw[pl.ds(r,n),:],mk[pl.ds(r,n),:]),write)
-        def body(i,_):
-            r=pl.ds(pl.multiple_of(i*80,16),80)
+        def rows(r):
             s=mid[r,:]
             st[r,:]=s.astype(BF)
             cc,rstd=row_stats(s)
-            n1[r,:]=(cc*rstd*vec_o[1:2,:]+vec_o[2:3,:]).astype(BF)
-            return 0
-        lax.fori_loop(0,10,body,0)
-        put(st,st_o)
+            xh=cc*rstd
+            xa[r,:]=xh.astype(BF); meta_o[r,2:3]=rstd
+            n1[r,:]=(xh*vec_o[1:2,:]+vec_o[2:3,:]).astype(BF)
+        by_sixteen(0,800,rows)
+        put(xa,xa_o)
     def cotangents():
+        loads[1].wait()
         raw[...]=cot_ref[...].astype(F32)
         def write2(r,n,v): mid[pl.ds(r,n),:]=v[0]
         settle_rows(g1,lambda r,n:(raw[pl.ds(r,n),:],),write2)
@@ -614,13 +621,13 @@
             mid[r,:]=st[r,:].astype(F32)+meta_o[r,0:1]*(nn(ctx[r,:],wpv)+vec_o[4:5,:])
             return 0
         lax.fori_loop(0,2,body,0)
-        def body(i,_):
-            r=pl.ds(pl.multiple_of(i*80,16),80)
+        def rows(r):
             cc,rstd=row_stats(mid[r,:])
-            n2[r,:]=(cc*rstd*vec_o[5:6,:]+vec_o[6:7,:]).astype(BF)
-            return 0
-        lax.fori_loop(0,10,body,0)
-        put(mid,mid_o)
+            xh=cc*rstd
+            xb[r,:]=xh.astype(BF); meta_o[r,3:4]=rstd
+            n2[r,:]=(xh*vec_o[5:6,:]+vec_o[6:7,:]).astype(BF)
+        by_sixteen(0,800,rows)
+        put(mid,mid_o); put(xb,xb_o)
         lag[0].wait(); outs[:]=[o for o in outs if o is not lag[0]]
         nt_[...]=n2[...].T
         put(nt_,n2_o)
@@ -672,15 +679,15 @@
     v=pltpu.VMEM
     R,W=tok.shape
     outs=[((3,4,4,48,768),BF),((4,4,48,768),BF),((4,4,48,3072),BF),((4,4,2,96,768),BF),((12,2,400,400),BF),
-        ((W,R),BF),((W,R),BF),((R,W),BF),((R,3*W),BF),((R,4*W),BF),((R,4*W),BF),((R,W),BF),((R,W),F32),((4,4,2,96,768),BF),((R,W),BF),((R,W),BF),
-        ((16,W),F32),((R,2),F32)]
+        ((W,R),BF),((W,R),BF),((R,W),BF),((R,3*W),BF),((R,4*W),BF),((R,4*W),BF),((R,W),BF),((R,W),BF),((R,W),F32),((4,4,2,96,768),BF),((R,W),BF),((R,W),BF),
+        ((16,W),F32),((R,4),F32)]
     return pl.pallas_call(forward_kernel,
-        in_specs=[M,M]+[V]*16,out_specs=[A]*16+[V,V],out_shape=[sds(*o) for o in outs],
+        in_specs=[M,M]+[V]*13+[A,A,V],out_specs=[A]*17+[V,V],out_shape=[sds(*o) for o in outs],
         scratch_shapes=[v((4,4,2,16,128),BF),v((3,4,4,48,768),BF),v((4,4,48,768),BF),v((4,4,48,3072),BF),
             v((24,2304),BF),v((24,768),BF),v((24,3072),BF),v((3,1,48,768),BF),v((1,48,768),BF),v((1,48,3072),BF),
-            v((R,W),F32),v((R,W),F32),v((R,W),BF),v((R,W),BF),v((W,R),BF),v((R,3*W),BF),v((2,400,400),F32),v((R,W),BF),v((R,W),BF),
-            v((R,4*W),BF),v((R,4*W),BF),v((R,W),BF),v((R,W),BF),v((4,4,2,96,768),BF),v((2,2,400,400),BF),v((2,400,400),F32),v((16,128),BF),v((16,128),F32),v((800,1),F32),v((1,2*W),F32),v((1,4*W),F32),
-            D((5,)),D((5,)),D((1,)),D((14,)),D((14,)),D((6,21)),D((6,21)),D((2,)),D((24,))],
+            v((R,W),F32),v((R,W),F32),v((R,W),BF),v((R,W),BF),v((R,W),BF),v((R,W),BF),v((W,R),BF),v((R,3*W),BF),v((2,400,400),F32),v((R,W),BF),v((R,W),BF),
+            v((R,4*W),BF),v((R,4*W),BF),v((R,W),BF),v((R,W),BF),v((4,4,2,96,768),BF),v((2,2,400,400),BF),v((2,400,400),F32),v((16,128),BF),v((16,128),F32),v((800,1),F32),v((R,W),BF),v((R,W),BF),v((1,2*W),F32),v((1,4*W),F32),
+            D((5,)),D((5,)),D((1,)),D((14,)),D((14,)),D((6,21)),D((6,21)),D((2,)),D((24,)),D((2,))],
         compiler_params=pltpu.CompilerParams(collective_id=0,has_side_effects=True,vmem_limit_bytes=60<<20),name="forward")(
         groups,offsets,*vectors,wq,wp,w1,w2,tok,cot,mask)
 
@@ -765,13 +772,13 @@
         for cp in self.cps: cp.wait_send()
 
 BACKWARD_ORDER=(
-    0, 200, 16, 240, 1, 241, 242, 243, 2, 220, 221, 32, 17, 48, 222, 223, 49, 201, 64, 33, 18, 3, 80, 202, 50, 203,
-    204, 65, 96, 250, 81, 19, 34, 97, 251, 230, 112, 66, 252, 113, 51, 253, 35, 98, 67, 82, 231, 114, 128, 254,
-    129, 83, 99, 255, 130, 232, 176, 144, 36, 52, 4, 115, 131, 177, 205, 178, 145, 206, 179, 207, 160, 146, 132,
-    161, 116, 147, 162, 208, 163, 84, 20, 209, 100, 68, 180, 148, 164,
+    0, 200, 240, 241, 242, 16, 1, 243, 220, 221, 17, 222, 64, 32, 48, 223, 2, 201, 33, 65, 18, 202, 80, 49, 203,
+    3, 34, 204, 250, 251, 81, 96, 19, 230, 112, 50, 252, 66, 35, 82, 97, 253, 231, 83, 113, 51, 254, 67, 128, 98,
+    114, 255, 129, 232, 176, 99, 115, 4, 36, 144, 130, 177, 205, 131, 178, 145, 206, 179, 207, 160, 146, 161, 147,
+    84, 162, 208, 163, 68, 20, 100, 52, 116, 132, 148, 209, 180, 164,
 )
 
-def backward_kernel(w2_r,w1_r,wp_r,wq_r,pr_r,n1_r,n2_r,ctx_r,pj_r,hid_r,dg_r,st_r,mid_r,pt2_r,gt_r,cs_r,vec,meta,
+def backward_kernel(w2_r,w1_r,wp_r,wq_r,pr_r,n1_r,n2_r,ctx_r,pj_r,hid_r,dg_r,xa_r,xb_r,mid_r,pt2_r,gt_r,cs_r,vec,meta,
         out_o,tok_o,sm_o,oq,op_,o1,o2,
         w2,w1,wp,gp,pj,mid,gf,nt_,tmp,ctx,gt,gb,pst,acc,accb,
         a2,s2,xa2,yb2,x2,y2,b2,z2,part,sb,xab,ybb,xb,yb,bb,zb,fb,frb,vs,vr,us,ur,
@@ -791,12 +798,12 @@
     CH=[Reduce(part.at[i,:,:,:,theirs],lambda zs,q,i=i: part.at[i,zs,q,:,mine],sib_at(i),xab.at[i],ybb.at[i],xb.at[i],yb.at[i],bb.at[i],zb.at[i],rss.at[2+i],rrs.at[2+i]) for i in range(8)]
     F=CH[0:4]; PJ=CH[4]; QK=CH[5:8]
     get("gt",gt_r,gt)
-    get("w2a",w2_r.at[pl.ds(0,32)],w2.at[pl.ds(0,32)]); get("dga",dg_r.at[:,pl.ds(0,1536)],gp.at[:,pl.ds(0,1536)])
-    get("a2a",pt2_r.at[:,:,c,0],a2.at[0])
-    get("w2b",w2_r.at[pl.ds(32,32)],w2.at[pl.ds(32,32)]); get("dgb",dg_r.at[:,pl.ds(1536,1536)],gp.at[:,pl.ds(1536,1536)])
-    get("a2b",pt2_r.at[:,:,c,1],a2.at[1])
-    get("n2",n2_r,nt_); get("cs",cs_r,tmp)
-    get("w1",w1_r,w1); get("mid",mid_r,mid); get("wp",wp_r,wp); get("ctx",ctx_r,ctx); get("pj",pj_r,pj)
+    def tile(i):
+        get("t%d"%i,w2_r.at[pl.ds(16*i,16)],w2.at[pl.ds(16*i,16)]); get("d%d"%i,dg_r.at[:,pl.ds(768*i,768)],gp.at[:,pl.ds(768*i,768)])
+    tile(0); tile(1)
+    ahead={240:lambda:(get("a2a",pt2_r.at[:,:,c,0],a2.at[0]),tile(2)),241:lambda:(tile(3),get("a2b",pt2_r.at[:,:,c,1],a2.at[1])),
+        242:lambda:get("n2",n2_r,nt_),243:lambda:(get("cs",cs_r,tmp),get("w1",w1_r,w1)),220:lambda:(get("xb",xb_r,gb),get("wp",wp_r,wp)),
+        221:lambda:get("ctx",ctx_r,ctx),222:lambda:get("pj",pj_r,pj)}
     acc[...]=jnp.zeros_like(acc)
     ends=[]
     def end(i):
@@ -813,34 +820,36 @@
         return 0
     def w1grad(i):
         have("n2")
+        if 220+i in ahead: ahead[220+i]()
         part[i]=nn(nt_[...],gp[:,768*i:768*i+768]).astype(BF).reshape(4,4,48,768)
         if i==3: get("n1",n1_r,nt_)
-    def norm_back(i0,rows,gain,ka,kb,finish):
+    def norm_back(i0,rows,col,gain,ka,kb,finish):
         def body(i,_):
-            r=pl.ds(pl.multiple_of(i0+i*80,16),80)
-            g,m=gf[r,:],rows(r)
-            cc,rstd=row_stats(m)
-            xh=cc*rstd
-            acc[ka]+=eights(g*xh); acc[kb]+=eights(g)
-            gx=g*gain
-            m1=jnp.sum(gx,axis=1,keepdims=True)*(1.0/768); m2=jnp.sum(gx*xh,axis=1,keepdims=True)*(1.0/768)
-            finish(r,rstd*(gx-m1-xh*m2))
+            sums={}; later=[]
+            def add(k,v): sums[k]=sums[k]+eights(v) if k in sums else eights(v)
+            for u in range(5):
+                r=pl.ds(pl.multiple_of(i0+(i*5+u)*16,16),16)
+                g,xh,rstd=gf[r,:],rows[r,:].astype(F32),meta[r,col:col+1]
+                add(ka,g*xh); add(kb,g)
+                gx=g*gain
+                m1=jnp.sum(gx,axis=1,keepdims=True)*(1.0/768); m2=jnp.sum(gx*xh,axis=1,keepdims=True)*(1.0/768)
+                later+=finish(r,rstd*(gx-m1-xh*m2),add)
+            for ref,r,v in later: ref[r,:]=v
+            for k,v in sums.items(): acc[k]+=v
             return 0
-        lax.fori_loop(0,5,body,0)
-    def finish2(r,d):
+        lax.fori_loop(0,25//5,body,0)
+    def finish2(r,d,add):
         gm=tmp[r,:].astype(F32)+d
-        mid[r,:]=gm
         v=(meta[r,0:1]*gm).astype(BF)
-        gb[r,:]=v
-        acc[4]+=eights(v.astype(F32))
-        acc[8]+=eights(gt[r,:].astype(F32))
+        add(4,v.astype(F32)); add(8,gt[r,:].astype(F32))
+        return [(mid,r,gm),(gb,r,v)]
     def p10(k):
-        have("w1","cs","mid")
+        have("w1","cs","xb")
         r=slice(400*k,400*k+400)
         gf[r,:]=nt(gp[r,:],w1[...].reshape(768,3072))
-        norm_back(400*k,lambda r: mid[r,:],vec[5:6,:],5,6,finish2)
+        norm_back(400*k,gb,3,vec[5:6,:],5,6,finish2)
         if k==1:
-            get("hid",hid_r,gp); get("st",st_r,tmp)
+            get("hid",hid_r,gp); get("xa",xa_r,tmp)
             for g in range(3): get("wq%d"%g,wq_r.at[g],w1.at[:,:,:,pl.ds(768*g,768)])
     gc=gt
     def gctx():
@@ -888,19 +897,19 @@
             for k in range(6): us[0,k:k+1,:]=jnp.sum(acc[3+k],axis=0,keepdims=True)
             for k in range(4): us[0,6+k:7+k,:]=jnp.sum(accb[:,768*k:768*k+768],axis=0,keepdims=True)
             us[0,10:16,:]=jnp.zeros((6,768),F32)
-    def finish1(r,d):
+    def finish1(r,d,add):
         gs=mid[r,:]+d
         m=meta[r,1:2]>0.0
-        acc[0]+=eights(jnp.where(m,gs,0.0))
-        mid[r,:]=jnp.where(m,0.0,gs)
+        add(0,jnp.where(m,gs,0.0))
+        return [(mid,r,jnp.where(m,0.0,gs))]
     stores=[]
     def put(src,dst):
         cp=pltpu.make_async_copy(src,dst,osem.at[len(stores)]); cp.start(); stores.append(cp)
     def back(i):
-        if i==0: have("st","wq0","wq1","wq2")
+        if i==0: have("xa","wq0","wq1","wq2")
         r=slice(400*i,400*i+400)
         gf[r,:]=sum(nt(group(r,g),w1[:,:,:,768*g:768*g+768].reshape(768,768)) for g in range(3))
-        norm_back(400*i,lambda r: tmp[r,:].astype(F32),vec[1:2,:],1,2,finish1)
+        norm_back(400*i,tmp,2,vec[1:2,:],1,2,finish1)
         if i==1: put(mid,tok_o); get("mid2",mid_r,gf)
     def fin():
         for k in range(3): vs[0,k:k+1,:]=jnp.sum(acc[k],axis=0,keepdims=True)
@@ -932,11 +941,10 @@
             a=b=op%10
             while k<len(BACKWARD_ORDER) and BACKWARD_ORDER[k]==op-a+b+1: b+=1; k+=1
             if op<250:
+                have("gt")
                 for i in range(a,b+1):
-                    if i==0: have("gt","w2a","dga")
-                    if i==2: have("w2b","dgb")
-                for lo,hi in ((a,min(b+1,2)),(max(a,2),b+1)):
-                    if lo<hi: lax.fori_loop(lo,hi,mlp,0)
+                    have("t%d"%i,"d%d"%i); ahead[240+i]()
+                    lax.fori_loop(i,i+1,mlp,0)
             else:
                 if a==0: have("pj")
                 lax.fori_loop(2*a,2*b+2,attend,0)
@@ -965,7 +973,7 @@
     for cp in stores: cp.wait()
     for q in C2+CH+sums: q.drain()
 
-def backward(w2,w1,wp,wq,pr,n1,n2,ctx,pj,hid,dg,st,mid,pt2,gt,cs,vec,meta):
+def backward(w2,w1,wp,wq,pr,n1,n2,ctx,pj,hid,dg,xa,xb,mid,pt2,gt,cs,vec,meta):
     sds=jax.ShapeDtypeStruct
     V=pl.BlockSpec(memory_space=pltpu.VMEM); A=pl.BlockSpec(memory_space=pl.ANY)
     D=pltpu.SemaphoreType.DMA
@@ -978,33 +986,40 @@
         return o
     scr+=rs(2,48,W,W)+rs(8,48,W//2,W)
     scr+=[v((8,2,24,W//2),F32),v((8,24,W//2),F32),v((4,8,W),F32),v((6,8,W),F32),v((4,16,W),F32),v((6,16,W),F32)]
-    scr+=[D((24,)),D((2,)),D((3,)),D((10,10)),D((10,10)),D((8,)),D((8,))]+[D((6,))]*4
+    scr+=[D((28,)),D((2,)),D((3,)),D((10,10)),D((10,10)),D((8,)),D((8,))]+[D((6,))]*4
     outs=[((R,W),F32),((R,W),F32),((16,128),F32),((24,3*W),F32),((24,W),F32),((24,4*W),F32),((96,W),F32)]
-    return pl.pallas_call(backward_kernel,in_specs=[A]*16+[V]*2,out_specs=[A,A]+[V]*5,out_shape=[sds(*o) for o in outs],scratch_shapes=scr,
+    return pl.pallas_call(backward_kernel,in_specs=[A]*17+[V]*2,out_specs=[A,A]+[V]*5,out_shape=[sds(*o) for o in outs],scratch_shapes=scr,
         compiler_params=pltpu.CompilerParams(collective_id=1,has_side_effects=True,vmem_limit_bytes=63<<20),name="backward")(
-        w2,w1,wp,wq,pr,n1,n2,ctx,pj,hid,dg,st,mid,pt2,gt,cs,vec,meta)
-
-def settle_back_kernel(groups,out_r,tok_r,sm,q_r,p_r,w1_r,w2_r,out_o,tok_o,q_o,p_o,w1_o,w2_o,v0,v1,v2,v3,v4,v5,v6,v7,v8,buf,sem):
-    cps=[pltpu.make_async_copy(a,b,sem.at[i]) for i,(a,b) in enumerate(((out_r,buf),(q_r,q_o),(p_r,p_o),(w1_r,w1_o),(w2_r,w2_o)))]
-    for cp in cps: cp.start()
+        w2,w1,wp,wq,pr,n1,n2,ctx,pj,hid,dg,xa,xb,mid,pt2,gt,cs,vec,meta)
+
+def settle_back_kernel(groups,out_r,tok_r,sm,q_r,p_r,w1_r,w2_r,out_o,tok_o,q_o,p_o,w1_o,w2_o,v0,v1,v2,v3,v4,v5,v6,v7,v8,buf,ob,tb,qb,pb,b1,b2,sem):
+    pairs=((tok_r,tb),(out_r,buf),(w1_r,b1),(q_r,qb),(w2_r,b2),(p_r,pb))
+    loads=[pltpu.make_async_copy(a,b,sem.at[i]) for i,(a,b) in enumerate(pairs)]
+    for cp in loads: cp.start()
     moved=groups[0]==1
-    one=[pltpu.make_async_copy(tok_r,tok_o,sem.at[5])]
-    three=[pltpu.make_async_copy(tok_r.at[pl.ds(a,n)],tok_o.at[pl.ds(b,n)],sem.at[6+i]) for i,(a,b,n) in enumerate(((0,0,392),(400,392,400),(392,792,8)))]
+    one=[pltpu.make_async_copy(tb,tok_o,sem.at[6])]
+    three=[pltpu.make_async_copy(tb.at[pl.ds(a,n)],tok_o.at[pl.ds(b,n)],sem.at[7+i]) for i,(a,b,n) in enumerate(((0,0,392),(400,392,400),(392,792,8)))]
+    for i,v in enumerate((v0,v1,v2,v3,v4,v5,v6,v7,v8)):
+        m=v.shape[0]
+        v[...]=sm[i:i+1,0:m].reshape(m)
+    loads[0].wait()
     @pl.when(moved)
     def _():
         for cp in three: cp.start()
     @pl.when(jnp.logical_not(moved))
     def _():
         for cp in one: cp.start()
-    for i,v in enumerate((v0,v1,v2,v3,v4,v5,v6,v7,v8)):
-        m=v.shape[0]
-        v[...]=sm[i:i+1,0:m].reshape(m)
-    cps[0].wait()
-    out_o[0:384]=buf[0:384].astype(BF)
+    loads[1].wait()
+    ob[0:384]=buf[0:384].astype(BF)
     a=buf[384:800]
     b=jnp.concatenate([buf[384:392],buf[400:800],buf[392:400]],axis=0)
-    out_o[384:800]=jnp.where(moved,b,a).astype(BF)
-    for cp in cps[1:]: cp.wait()
+    ob[384:800]=jnp.where(moved,b,a).astype(BF)
+    stores=[pltpu.make_async_copy(ob,out_o,sem.at[10])]
+    stores[0].start()
+    for i,(b,o) in enumerate(((b1,w1_o),(qb,q_o),(b2,w2_o),(pb,p_o))):
+        loads[2+i].wait()
+        cp=pltpu.make_async_copy(b,o,sem.at[11+i]); cp.start(); stores.append(cp)
+    for cp in stores: cp.wait()
     @pl.when(moved)
     def _():
         for cp in three: cp.wait()
@@ -1015,9 +1030,10 @@
 def settle_back(groups,sizes,out,tok,sm,q,p,w1,w2):
     sds=jax.ShapeDtypeStruct
     V=pl.BlockSpec(memory_space=pltpu.VMEM); A=pl.BlockSpec(memory_space=pl.ANY); M=pl.BlockSpec(memory_space=pltpu.SMEM)
-    return pl.pallas_call(settle_back_kernel,in_specs=[M,A,A,V,A,A,A,A],out_specs=[V]+[A]*5+[V]*len(sizes),
+    v=pltpu.VMEM
+    return pl.pallas_call(settle_back_kernel,in_specs=[M,A,A,V,A,A,A,A],out_specs=[A]*6+[V]*len(sizes),
         out_shape=[sds(out.shape,BF)]+[sds(a.shape,F32) for a in (tok,q,p,w1,w2)]+[sds((m,),F32) for m in sizes],
-        scratch_shapes=[pltpu.VMEM(out.shape,F32),pltpu.SemaphoreType.DMA((9,))],
+        scratch_shapes=[v(out.shape,F32),v(out.shape,BF)]+[v(a.shape,F32) for a in (tok,q,p,w1,w2)]+[pltpu.SemaphoreType.DMA((15,))],
         compiler_params=pltpu.CompilerParams(vmem_limit_bytes=60<<20),name="settle_back")(groups,out,tok,sm,q,p,w1,w2)
 
 def normalize(values, gain, shift):
@@ -1125,12 +1141,12 @@
            ln2_gain, ln2_bias, w_fc1, b_fc1, w_fc2, b_fc2, cotangent):
     vectors = (mask_token, ln1_gain, ln1_bias, b_qv, b_proj, ln2_gain, ln2_bias, b_fc1, b_fc2)
     sizes = [v.shape[0] for v in vectors]
-    (gq, gp, g1, g2, probs, normed_one, normed_two, context_low, projected, hidden_low, dgelu, start, middle, part2,
+    (gq, gp, g1, g2, probs, normed_one, normed_two, context_low, projected, hidden_low, dgelu, rows_one, rows_two, middle, part2,
      grad_two, cots, vec, meta) = forward(groups, offsets, vectors, w_qkv, w_proj, w_fc1, w_fc2, tokens, cotangent, mask_bits)
     width = tokens.shape[1]
     shares = backward(
         g2.reshape(64, 48, width), g1, gp, gq, probs, normed_one, normed_two, context_low,
-        projected, hidden_low, dgelu, start, middle, part2.reshape(4, 4, 2, 2, 48, width), grad_two, cots, vec, meta)
+        projected, hidden_low, dgelu, rows_one, rows_two, middle, part2.reshape(4, 4, 2, 2, 48, width), grad_two, cots, vec, meta)
     output, grad_input, share_qkv, share_proj, share_fc1, share_fc2, *v = settle_back(groups, sizes, *shares)
     return (output, grad_input, v[0], v[1], v[2], share_qkv, v[3], share_proj, v[4], v[5], v[6], share_fc1, v[7],
             share_fc2, v[8])

time: 277 us -> 177 us (0.64)
  Pallas kernels: 273 us -> 173 us
    pallas_call x1, Pallas kernels: 104 us -> 5.26 us  [settle_back(): pl.pallas_call(settle_back_kernel, in_specs=[M, A, A, V, A, A, A, A], out...]
where the time goes in v1:
time: 177 us; the launch traced here: 174 us
  Pallas kernels  173 us (98%)
    pallas_call x1, Pallas kernels, backward(): pl.pallas_call(backward_kernel, in_specs=[A] * 17 + [V] * 2, out_specs=[A...  90.5 us
    pallas_call x1, Pallas kernels, forward(): pl.pallas_call(forward_kernel, in_specs=[M, M] + [V] * 13 + [A, A, V], ou...  76.9 us
    pallas_call x1, Pallas kernels, settle_back(): pl.pallas_call(settle_back_kernel, in_specs=[M, A, A, V, A, A, A, A], out...  5.26 us

profile of v1, /device:TPU:0, one launch (start us, length us, event | category | flops | bytes accessed | tf_op | source)
XLA Modules:
  0.0 173.8 jit_solution(3204114849783194532)
XLA Ops:
  0.7 76.9 %forward.1 = (bf16[3,4,4,48,768]{4,3,2,1,0:T(8,128)(2,1)}, bf16[4,4,48,768]{3,2,1,0:T(8,128)(2,1)}, bf16[4,4,48,3072]{3,2,1,0:T(8,128)(2,1)}, bf16[4,4,2,96,768]...) custom-call(s32[8]{0:T(128)} %groups.3, ...), custom_call_target="tpu_custom_call" | custom-call | tf_op jit(solution)/shard_map/forward/pallas_call | solution.py:684
  77.5 90.5 %backward.1 = (f32[800,768]{1,0:T(8,128)}, f32[800,768]{1,0:T(8,128)}, f32[16,128]{1,0:T(8,128)}, f32[24,2304]{1,0:T(8,128)}, f32[24,768]{1,0:T(8,128)}, /*index=5*/f32[24,3072]{1,0:T(8,128)}, f32[96,768]{1,0:T(8,128)}) custom-call(bf16[64,48,768]{2,1,0:T(8,128)(2,1)} %bitcast.2, bf16[4,4,48,3072]{3,2,1,0:T(8,128)(2,1)} %get-tuple-element.57.w1_r, ...), custom_call_target="tpu_custom_call" | custom-call | tf_op jit(solution)/shard_map/backward/pallas_call | solution.py:991
  168.1 5.3 %settle_back.1 = (bf16[800,768]{1,0:T(8,128)(2,1)}, f32[800,768]{1,0:T(8,128)}, f32[24,2304]{1,0:T(8,128)}, f32[24,768]{1,0:T(8,128)}, f32[24,3072]{1,0:T(8,128)...) custom-call(s32[8]{0:T(128)} %groups.3, ...), custom_call_target="tpu_custom_call" | custom-call | tf_op jit(solution)/shard_map/settle_back/pallas_call | solution.py:1034

commit v2 on v1

--- a/solution.py
+++ b/solution.py
@@ -705,14 +705,11 @@
         cp.start(); self.cps[slot]=cp
     def r0(self): self.send(self.give,self.s,0,self.sd)
     def add(self,n,z0,yx,other):
-        def body(i,_):
-            t=self.a(pl.ds(i+z0,1),yx)
-            t[...]=t[...]+other(i)[...]
-            return 0
-        lax.fori_loop(0,n,body,0)
+        t=self.a(pl.ds(z0,n),yx)
+        t[...]=t[...]+other[...]
     def r1(self):
         self.cps[0].wait_recv()
-        def own(yx): self.add(4,0,yx,lambda i: self.s.at[pl.ds(i,1),yx])
+        def own(yx): self.add(4,0,yx,self.s.at[:,yx])
         own(self.dg)
         self.send(self.a(pl.ds(0,2),self.dg),self.rxa,1,self.xd)
         self.send(self.a(pl.ds(2,2),self.dg),self.ryb,2,self.yd)
@@ -723,18 +720,16 @@
         own(self.yx)
     def r2(self):
         self.cps[1].wait_recv()
-        self.add(2,0,self.yn,lambda i: self.rxa.at[pl.ds(i,1)])
+        self.add(2,0,self.yn,self.rxa)
         self.send(self.a(pl.ds(0,2),self.yn),self.ry.at[pl.ds(0,2)],6,self.yd)
         self.cps[2].wait_recv()
-        self.add(2,2,self.xn,lambda i: self.ryb.at[pl.ds(i,1)])
+        self.add(2,2,self.xn,self.ryb)
         self.send(self.a(pl.ds(2,2),self.xn),self.rx.at[pl.ds(2,2)],5,self.xd)
     def r3(self):
         for s in (3,4,5,6): self.cps[s].wait_recv()
-        def body(i,_):
+        for i in range(4):
             k=pl.ds(i,1)
             self.b[k]=(self.a(k,self.yx)[...].astype(F32)+self.rx[k].astype(F32)+self.ry[k].astype(F32)).astype(BF)
-            return 0
-        lax.fori_loop(0,4,body,0)
         for k in (1,2,3):
             zz=lax.rem(self.z+k,4)
             self.send(self.b.at[zz],self.rz.at[k-1],6+k,dev(zz,self.yx,self.c))
@@ -758,24 +753,25 @@
         cp.start(); self.cps.append(cp)
     def stage(self,k):
         c,x,y,z=place(); yx=y*2+x
-        if k:
-            if k<4: self.cps[k-1].wait_recv(); self.v[k]=self.v[k-1]+self.r[k-1]
         if k==0: self.send(0,0,dev(z,yx,1-c))
-        elif k==1: self.send(1,1,dev(z,y*2+1-x,c))
-        elif k==2: self.send(2,2,dev(z,(1-y)*2+x,c))
-        elif k==3:
-            for h in (1,2,3): self.send(3,2+h,dev(lax.rem(z+h,4),yx,c))
+        elif k==1:
+            self.cps[0].wait_recv(); self.v[1]=self.v[0]+self.r[0]
+            self.send(1,1,dev(z,y*2+1-x,c)); self.send(1,2,dev(z,(1-y)*2+x,c)); self.send(1,3,dev(z,(1-y)*2+1-x,c))
+        elif k==2:
+            for h in (1,2,3): self.cps[h].wait_recv()
+            self.v[2]=self.v[1]+self.r[1]+(self.r[2]+self.r[3])
+            for h in (1,2,3): self.send(2,3+h,dev(lax.rem(z+h,4),yx,c))
         else:
-            for h in (1,2,3): self.cps[2+h].wait_recv()
-            self.sum=self.v[3]+self.r[3]+self.r[4]+self.r[5]
+            for h in (1,2,3): self.cps[3+h].wait_recv()
+            self.sum=self.v[2]+self.r[4]+self.r[5]+self.r[6]
     def drain(self):
         for cp in self.cps: cp.wait_send()
 
 BACKWARD_ORDER=(
-    0, 200, 240, 241, 242, 16, 1, 243, 220, 221, 17, 222, 64, 32, 48, 223, 2, 201, 33, 65, 18, 202, 80, 49, 203,
-    3, 34, 204, 250, 251, 81, 96, 19, 230, 112, 50, 252, 66, 35, 82, 97, 253, 231, 83, 113, 51, 254, 67, 128, 98,
-    114, 255, 129, 232, 176, 99, 115, 4, 36, 144, 130, 177, 205, 131, 178, 145, 206, 179, 207, 160, 146, 161, 147,
-    84, 162, 208, 163, 68, 20, 100, 52, 116, 132, 148, 209, 180, 164,
+    16, 200, 240, 241, 242, 0, 17, 243, 220, 221, 222, 32, 1, 64, 223, 201, 18, 33, 202, 80, 48, 2, 203, 34, 204,
+    19, 96, 81, 250, 97, 3, 49, 251, 35, 230, 252, 112, 98, 82, 50, 65, 253, 113, 99, 231, 128, 83, 254, 51, 66,
+    255, 114, 232, 176, 129, 67, 115, 144, 177, 205, 130, 4, 68, 145, 100, 178, 206, 146, 131, 207, 160, 36, 84,
+    161, 147, 208, 116, 162, 209, 179, 148, 52, 20, 132, 163,
 )
 
 def backward_kernel(w2_r,w1_r,wp_r,wq_r,pr_r,n1_r,n2_r,ctx_r,pj_r,hid_r,dg_r,xa_r,xb_r,mid_r,pt2_r,gt_r,cs_r,vec,meta,
@@ -985,8 +981,8 @@
         o=[v((n,4,4,r,own),BF),v((min(n,5),4,4,r,w),BF),v((n,2,r,w),BF),v((n,2,r,w),BF),v((n,4,r,w),BF),v((n,4,r,w),BF),v((n,4,r,w),BF),v((n,3,r,w),BF)]
         return o
     scr+=rs(2,48,W,W)+rs(8,48,W//2,W)
-    scr+=[v((8,2,24,W//2),F32),v((8,24,W//2),F32),v((4,8,W),F32),v((6,8,W),F32),v((4,16,W),F32),v((6,16,W),F32)]
-    scr+=[D((28,)),D((2,)),D((3,)),D((10,10)),D((10,10)),D((8,)),D((8,))]+[D((6,))]*4
+    scr+=[v((8,2,24,W//2),F32),v((8,24,W//2),F32),v((3,8,W),F32),v((7,8,W),F32),v((3,16,W),F32),v((7,16,W),F32)]
+    scr+=[D((28,)),D((2,)),D((3,)),D((10,10)),D((10,10)),D((8,)),D((8,))]+[D((7,))]*4
     outs=[((R,W),F32),((R,W),F32),((16,128),F32),((24,3*W),F32),((24,W),F32),((24,4*W),F32),((96,W),F32)]
     return pl.pallas_call(backward_kernel,in_specs=[A]*17+[V]*2,out_specs=[A,A]+[V]*5,out_shape=[sds(*o) for o in outs],scratch_shapes=scr,
         compiler_params=pltpu.CompilerParams(collective_id=1,has_side_effects=True,vmem_limit_bytes=63<<20),name="backward")(

time: 177 us -> 174 us (0.983)
  Pallas kernels: 173 us -> 170 us
    pallas_call x1, Pallas kernels: 90.5 us -> 88.2 us  [backward(): pl.pallas_call(backward_kernel, in_specs=[A] * 17 + [V] * 2, out_specs=[A...]
where the time goes in v2:
time: 174 us; the launch traced here: 171 us
  Pallas kernels  170 us (98%)
    pallas_call x1, Pallas kernels, backward(): pl.pallas_call(backward_kernel, in_specs=[A] * 17 + [V] * 2, out_specs=[A...  88.2 us
    pallas_call x1, Pallas kernels, forward(): pl.pallas_call(forward_kernel, in_specs=[M, M] + [V] * 13 + [A, A, V], ou...  76.9 us
    pallas_call x1, Pallas kernels, settle_back(): pl.pallas_call(settle_back_kernel, in_specs=[M, A, A, V, A, A, A, A], out...  5.25 us

profile of v2, /device:TPU:0, one launch (start us, length us, event | category | flops | bytes accessed | tf_op | source)
XLA Modules:
  0.0 171.2 jit_solution(2981108175667284265)
XLA Ops:
  0.7 76.9 %forward.1 = (bf16[3,4,4,48,768]{4,3,2,1,0:T(8,128)(2,1)}, bf16[4,4,48,768]{3,2,1,0:T(8,128)(2,1)}, bf16[4,4,48,3072]{3,2,1,0:T(8,128)(2,1)}, bf16[4,4,2,96,768]...) custom-call(s32[8]{0:T(128)} %groups.3, ...), custom_call_target="tpu_custom_call" | custom-call | tf_op jit(solution)/shard_map/forward/pallas_call | solution.py:684
  77.5 88.2 %backward.1 = (f32[800,768]{1,0:T(8,128)}, f32[800,768]{1,0:T(8,128)}, f32[16,128]{1,0:T(8,128)}, f32[24,2304]{1,0:T(8,128)}, f32[24,768]{1,0:T(8,128)}, /*index=5*/f32[24,3072]{1,0:T(8,128)}, f32[96,768]{1,0:T(8,128)}) custom-call(bf16[64,48,768]{2,1,0:T(8,128)(2,1)} %bitcast.2, bf16[4,4,48,3072]{3,2,1,0:T(8,128)(2,1)} %get-tuple-element.57.w1_r, ...), custom_call_target="tpu_custom_call" | custom-call | tf_op jit(solution)/shard_map/backward/pallas_call | solution.py:987
  165.7 5.3 %settle_back.1 = (bf16[800,768]{1,0:T(8,128)(2,1)}, f32[800,768]{1,0:T(8,128)}, f32[24,2304]{1,0:T(8,128)}, f32[24,768]{1,0:T(8,128)}, f32[24,3072]{1,0:T(8,128)...) custom-call(s32[8]{0:T(128)} %groups.3, ...), custom_call_target="tpu_custom_call" | custom-call | tf_op jit(solution)/shard_map/settle_back/pallas_call | solution.py:1030

commit v3 on v2

--- a/solution.py
+++ b/solution.py
@@ -913,8 +913,8 @@
     def outp(i):
         if i==0: have("hid","mid2")
         r=slice(400*i,400*i+400)
-        gf[r,:]=gf[r,:]+meta[r,0:1]*(nn(gp[r,:],w2[...].reshape(3072,768))+vec[8:9,:])
-        put(gf.at[pl.ds(400*i,400)],out_o.at[pl.ds(400*i,400)])
+        gb[r,:]=(gf[r,:]+meta[r,0:1]*(nn(gp[r,:],w2[...].reshape(3072,768))+vec[8:9,:])).astype(BF)
+        put(gb.at[pl.ds(400*i,400)],out_o.at[pl.ds(400*i,400)])
     sums=[Total(vs,vr,vss,vrs),Total(us,ur,uss,urs)]
     plain=(lambda:None,lambda:p10(0),lambda:p10(1),gctx,wpgrad,lambda:back(0),lambda:back(1),fin,lambda:outp(0),lambda:outp(1))
     k=0
@@ -983,7 +983,7 @@
     scr+=rs(2,48,W,W)+rs(8,48,W//2,W)
     scr+=[v((8,2,24,W//2),F32),v((8,24,W//2),F32),v((3,8,W),F32),v((7,8,W),F32),v((3,16,W),F32),v((7,16,W),F32)]
     scr+=[D((28,)),D((2,)),D((3,)),D((10,10)),D((10,10)),D((8,)),D((8,))]+[D((7,))]*4
-    outs=[((R,W),F32),((R,W),F32),((16,128),F32),((24,3*W),F32),((24,W),F32),((24,4*W),F32),((96,W),F32)]
+    outs=[((R,W),BF),((R,W),F32),((16,128),F32),((24,3*W),F32),((24,W),F32),((24,4*W),F32),((96,W),F32)]
     return pl.pallas_call(backward_kernel,in_specs=[A]*17+[V]*2,out_specs=[A,A]+[V]*5,out_shape=[sds(*o) for o in outs],scratch_shapes=scr,
         compiler_params=pltpu.CompilerParams(collective_id=1,has_side_effects=True,vmem_limit_bytes=63<<20),name="backward")(
         w2,w1,wp,wq,pr,n1,n2,ctx,pj,hid,dg,xa,xb,mid,pt2,gt,cs,vec,meta)
@@ -1006,9 +1006,9 @@
     def _():
         for cp in one: cp.start()
     loads[1].wait()
-    ob[0:384]=buf[0:384].astype(BF)
-    a=buf[384:800]
-    b=jnp.concatenate([buf[384:392],buf[400:800],buf[392:400]],axis=0)
+    ob[0:384]=buf[0:384]
+    a=buf[384:800].astype(F32)
+    b=jnp.concatenate([a[0:8],a[16:416],a[8:16]],axis=0)
     ob[384:800]=jnp.where(moved,b,a).astype(BF)
     stores=[pltpu.make_async_copy(ob,out_o,sem.at[10])]
     stores[0].start()
@@ -1029,7 +1029,7 @@
     v=pltpu.VMEM
     return pl.pallas_call(settle_back_kernel,in_specs=[M,A,A,V,A,A,A,A],out_specs=[A]*6+[V]*len(sizes),
         out_shape=[sds(out.shape,BF)]+[sds(a.shape,F32) for a in (tok,q,p,w1,w2)]+[sds((m,),F32) for m in sizes],
-        scratch_shapes=[v(out.shape,F32),v(out.shape,BF)]+[v(a.shape,F32) for a in (tok,q,p,w1,w2)]+[pltpu.SemaphoreType.DMA((15,))],
+        scratch_shapes=[v(out.shape,BF),v(out.shape,BF)]+[v(a.shape,F32) for a in (tok,q,p,w1,w2)]+[pltpu.SemaphoreType.DMA((15,))],
         compiler_params=pltpu.CompilerParams(vmem_limit_bytes=60<<20),name="settle_back")(groups,out,tok,sm,q,p,w1,w2)
 
 def normalize(values, gain, shift):

time: 174 us -> 174 us (level)
  no operation moved by 1% of the time
where the time goes in v3:
time: 174 us; the launch traced here: 171 us
  Pallas kernels  170 us (98%)
    pallas_call x1, Pallas kernels, backward(): pl.pallas_call(backward_kernel, in_specs=[A] * 17 + [V] * 2, out_specs=[A...  88.2 us
    pallas_call x1, Pallas kernels, forward(): pl.pallas_call(forward_kernel, in_specs=[M, M] + [V] * 13 + [A, A, V], ou...  76.9 us
    pallas_call x1, Pallas kernels, settle_back(): pl.pallas_call(settle_back_kernel, in_specs=[M, A, A, V, A, A, A, A], out...  5.2 us

profile of v3, /device:TPU:0, one launch (start us, length us, event | category | flops | bytes accessed | tf_op | source)
XLA Modules:
  0.0 171.2 jit_solution(11940206721201809788)
XLA Ops:
  0.7 76.9 %forward.1 = (bf16[3,4,4,48,768]{4,3,2,1,0:T(8,128)(2,1)}, bf16[4,4,48,768]{3,2,1,0:T(8,128)(2,1)}, bf16[4,4,48,3072]{3,2,1,0:T(8,128)(2,1)}, bf16[4,4,2,96,768]...) custom-call(s32[8]{0:T(128)} %groups.3, ...), custom_call_target="tpu_custom_call" | custom-call | tf_op jit(solution)/shard_map/forward/pallas_call | solution.py:684
  77.5 88.2 %backward.1 = (bf16[800,768]{1,0:T(8,128)(2,1)}, f32[800,768]{1,0:T(8,128)}, f32[16,128]{1,0:T(8,128)}, f32[24,2304]{1,0:T(8,128)}, f32[24,768]{1,0:T(8,128)}, /*index=5*/f32[24,3072]{1,0:T(8,128)}, f32[96,768]{1,0:T(8,128)}) custom-call(bf16[64,48,768]{2,1,0:T(8,128)(2,1)} %bitcast.2, bf16[4,4,48,3072]{3,2,1,0:T(8,128)(2,1)} %get-tuple-element.57.w1_r, ...), custom_call_target="tpu_custom_call" | custom-call | tf_op jit(solution)/shard_map/backward/pallas_call | solution.py:987
  165.7 5.2 %settle_back.1 = (bf16[800,768]{1,0:T(8,128)(2,1)}, f32[800,768]{1,0:T(8,128)}, f32[24,2304]{1,0:T(8,128)}, f32[24,768]{1,0:T(8,128)}, f32[24,3072]{1,0:T(8,128)...) custom-call(s32[8]{0:T(128)} %groups.3, ...), custom_call_target="tpu_custom_call" | custom-call | tf_op jit(solution)/shard_map/settle_back/pallas_call | solution.py:1030
